TPU v7x, 32 devices: a whole 2x2x4 slice. The times are simulated.
32 devices in a mesh: ctx: 8 (over z, y), mp: 4 (over x, core).
Axes of the slice: x: 2, y: 2, z: 4, core: 2. Of those that a mesh axis runs over, the one named last changes fastest.
Arguments:
- features: bfloat16 [4096, 3, 8192], P('ctx', None, 'mp'), may hold values from -6 to 6
- residual: bfloat16 [4096, 8192], P('ctx', 'mp')
- short_taps: float32 [3, 7, 8192], P(None, None, 'mp'), may hold values from -2 to 2
- rates: float32 [512, 16], P('mp'), may hold values from 7.324219e-05 to 0.05, as said below
- residues: float32 [512, 16], P('mp'), may hold values from -4 to 4
- skip: float32 [8192], P('mp'), may hold values from -4 to 4
- gain: float32 [8192], P('mp'), may hold values from 0.5 to 1.5
- lengths: int32 [8], replicated, may hold values from 1 to 2048, 4096 in all
- owner: int32 [64], replicated, may hold values from 0 to 7, as said below
Outputs:
- relaid: bfloat16 [4096, 8192], P('ctx', 'mp')
Inputs may be any that keep to these rules, and one draw needn't show every extreme that they name: The owner of block i of index s is (s + o_i) mod 8 for offsets o_i that depend on i alone; exactly two of the 8 offsets are equal and the others differ, so every owner receives one block of each index i and at most 2 blocks come from one index to one owner. `rates`: every rate is positive.
All inputs are finite; a program needn't handle non-finite values.
Results may differ from a plain program's by a relative error of at most 0.0065.
Values may be sent and summed in bfloat16 or wider, within the bound.
No kernel may reach another device: no remote copies, remote signals or barrier semaphores. Data moves between devices by JAX's collectives and lax.ppermute only.
A program may use at most 128 MiB of HBM per device.

v0:
```python
import functools
import math

import jax
import jax.numpy as jnp
from jax import lax
from jax.experimental import pallas as pl
from jax.experimental.pallas import tpu as pltpu
from jax.sharding import PartitionSpec as P

SHORT = 7
LANES = 128
CHUNK = 128
HALO = 8
EPS = 1e-06
SPLIT = (3, 5)
WIDE = 512
SPAN = 64
F32 = jnp.float32
BF16 = jnp.bfloat16
VMEM_LIMIT = 60 * 1024 * 1024


def iota(shape, dim):
    return lax.broadcasted_iota(jnp.int32, shape, dim)


def document(ends, positions):
    total = jnp.zeros(positions.shape, jnp.int32)
    for end in ends:
        total = total + (positions >= end).astype(jnp.int32)
    return total


def scalar_document(ends, position):
    total = jnp.int32(0)
    for end in ends:
        total = total + (position >= end).astype(jnp.int32)
    return jnp.where(position < 0, -1, total)


def running_ends(lengths_ref, ndoc):
    ends, total = [], jnp.int32(0)
    for j in range(ndoc):
        total = total + lengths_ref[j]
        ends.append(total)
    return ends


def write_lag_masks(mask_ref, ends, base, count):
    mask_ref[...] = jnp.ones_like(mask_ref)
    gap = jnp.zeros((1, LANES), F32)
    for end in ends:
        row = end - base + HALO

        @pl.when((row >= 0) & (row < count + HALO))
        def _(row=row):
            for lag in (1, 2, 3):
                for past in range(lag):
                    mask_ref[lag - 1, pl.ds(row + past, 1), :] = gap


def row_documents(ends, base, count):
    return document(ends, base + iota((8, count), 1)).astype(F32)


def is_second(owner_ref, nblocks, i):
    found = jnp.bool_(False)
    for j in range(i):
        found = found | (owner_ref[j] == owner_ref[i])
    return found


def write_slots(slot_ref, owner_ref, where, nblocks):
    unused = jnp.int32(nblocks * (nblocks - 1) // 2)
    seconds = [is_second(owner_ref, nblocks, i) for i in range(nblocks)]
    mine = [owner_ref[where * nblocks + i] for i in range(nblocks)]
    for i in range(nblocks):
        unused = unused - jnp.where(seconds[i], 0, mine[i])
    for i in range(nblocks):
        slot_ref[i] = jnp.where(seconds[i], unused, mine[i])
    slot_ref[nblocks] = unused


def tile_rates(rates_ref, low, size):
    first = low // size
    columns = [rates_ref[:, first + g : first + g + 1] for g in range(LANES // size)]
    return jnp.concatenate([jnp.broadcast_to(column, (column.shape[0], LANES)) for column in columns], 0)


def short_conv(ext, taps, masks):
    def back(value, lag):
        return pltpu.roll(value, lag, 0) * masks[lag - 1]

    one, two = back(ext, 1), back(ext, 2)
    far = ext * taps[6]
    middle = ext * taps[3] + one * taps[4] + two * taps[5] + back(far, 3)
    near = ext * taps[0] + one * taps[1] + two * taps[2] + back(middle, 3)
    return near[HALO:]


def extended(x_ref, halo_ref, which, start, lanes):
    rows = x_ref[0, start : start + SPAN, lanes].astype(F32)
    if start == 0:
        ahead = halo_ref[which, :, lanes].astype(F32)
    else:
        ahead = x_ref[0, start - 16 : start, lanes].astype(F32)[16 - HALO :]
    return jnp.concatenate([ahead, rows], 0)


def tap_rows(taps_ref, which, lanes):
    return [taps_ref[which, j : j + 1, lanes] for j in range(SHORT)]


def lag_masks(mask_ref, start):
    return [mask_ref[l, start : start + SPAN + HALO, :] for l in range(3)]


def group_mask(modes, size):
    return (iota((LANES, LANES), 0) // modes) == (iota((LANES, LANES), 1) // size)


def each_tile(width, body):
    for low in range(0, width, LANES):
        body(slice(low, low + LANES))


def mix_kernel(
    modes, size, ndoc,
    where_ref, lengths_ref,
    key_ref, value_ref, halo_ref, taps_ref, rates_ref,
    mixed_ref, state_ref,
    mask_ref, tail_ref,
):
    _, count, width = key_ref.shape
    chunks = count // CHUNK

    @pl.when(pl.program_id(0) == 0)
    def _():
        base = where_ref[0] * count
        ends = running_ends(lengths_ref, ndoc)
        write_lag_masks(mask_ref, ends, base, count)
        last = scalar_document(ends, base + count - 1).astype(F32)
        tail_ref[...] = jnp.where(row_documents(ends, base, count) == last, 1.0, 0.0).astype(F32)

    def tile(lanes):
        key_taps, value_taps = tap_rows(taps_ref, 1, lanes), tap_rows(taps_ref, 2, lanes)
        for start in range(0, count, SPAN):
            masks = lag_masks(mask_ref, start)
            key = short_conv(extended(key_ref, halo_ref, 1, start, lanes), key_taps, masks)
            value = short_conv(extended(value_ref, halo_ref, 2, start, lanes), value_taps, masks)
            mixed_ref[start : start + SPAN, lanes] = (key * value).astype(BF16)
        rate = tile_rates(rates_ref.at[0], lanes.start, size)
        leave = jnp.exp(-rate * (CHUNK - 1 - iota((LANES, CHUNK), 1)).astype(F32))
        whole = jnp.exp(-rate * CHUNK)
        spans = []
        for chunk in reversed(range(chunks)):
            tail = tail_ref[0:1, chunk * CHUNK : (chunk + 1) * CHUNK]
            spans.append((leave * tail).astype(BF16))
            leave = leave * whole
        full = jnp.dot(jnp.concatenate(spans[::-1], 1), mixed_ref[:, lanes], preferred_element_type=F32)
        full = jnp.where(group_mask(modes, size), full, 0.0)
        state = jnp.sum(full.reshape(LANES // modes, modes, LANES), 0).astype(BF16)
        for owner in range(state_ref.shape[0]):
            state_ref[owner, :, lanes] = state

    each_tile(width, tile)


def left_state(states_ref, flags_ref, rate, lanes, modes, size, count):
    inside = group_mask(modes, size)
    where = flags_ref[1]

    def gather(v, total):
        weight = jnp.exp(-rate * ((where - 1 - v) * count).astype(F32))
        piece = jnp.concatenate([states_ref[v, :, lanes].astype(F32)] * (LANES // modes), 0)
        return total + jnp.where(inside, piece * weight, 0.0)

    return lax.fori_loop(flags_ref[0], where, gather, jnp.zeros((LANES, LANES), F32))


def write_flags(flags_ref, ends, where, count, nblocks):
    before = scalar_document(ends, where * count - 1)
    first = jnp.int32(0)
    for v in range(nblocks):
        first = first + (scalar_document(ends, (v + 1) * count - 1) < before).astype(jnp.int32)
    flags_ref[0] = first
    flags_ref[1] = where
    for chunk in range(count // CHUNK):
        start = where * count + chunk * CHUNK
        held = scalar_document(ends, start - 1) == scalar_document(ends, start + CHUNK - 1)
        flags_ref[2 + chunk] = held.astype(jnp.int32)


def hand_over(out_ref, squares_ref, slot_ref, summed, start, rows, lanes):
    squares_ref[start : start + SPAN, :] += summed * summed
    rounded = summed.astype(BF16)
    for b in range(SPAN // rows):
        out_ref[slot_ref[start // rows + b], :, lanes] = rounded[b * rows : (b + 1) * rows]


def conv_kernel(modes, size, ndoc, nblocks, carried, where_ref, lengths_ref, owner_ref, *refs):
    x_ref, halo_ref, taps_ref, mixed_ref, rates_ref, residues_ref, skip_ref, residual_ref = refs[:8]
    refs = refs[8:]
    if carried:
        states_ref, out_ref, spare_ref, squares_ref = refs[:4]
        refs = refs[4:]
    else:
        base_ref, gate_ref = refs[:2]
        refs = refs[2:]
    mask_ref, same_ref, keep_ref, tail_ref, flags_ref = refs[:5]
    count, width = mixed_ref.shape
    chunks = count // CHUNK

    @pl.when(pl.program_id(0) == 0)
    def _():
        where = where_ref[0]
        base = where * count
        ends = running_ends(lengths_ref, ndoc)
        write_lag_masks(mask_ref, ends, base, count)
        write_flags(flags_ref, ends, where, count, nblocks)
        if carried:
            write_slots(refs[5], owner_ref, where, nblocks)
            squares_ref[...] = jnp.zeros_like(squares_ref)
        documents = row_documents(ends, base, count)
        causal = iota((CHUNK, CHUNK), 1) <= iota((CHUNK, CHUNK), 0)
        for chunk in range(chunks):
            start = base + chunk * CHUNK
            there = jnp.broadcast_to(documents[0:1, chunk * CHUNK : (chunk + 1) * CHUNK], (CHUNK, CHUNK))
            here = there.T
            same_ref[chunk] = jnp.where((here == there) & causal, 1.0, 0.0).astype(BF16)
            before = scalar_document(ends, start - 1).astype(F32)
            keep_ref[chunk] = jnp.where(here == before, 1.0, 0.0).astype(BF16)
            last = scalar_document(ends, start + CHUNK - 1).astype(F32)
            tail_ref[chunk] = jnp.where(there == last, 1.0, 0.0).astype(F32)

    groups = LANES // modes

    def tile(lanes):
        rate = tile_rates(rates_ref.at[0], lanes.start, size)
        scale = tile_rates(residues_ref.at[0], lanes.start, size) * jnp.sqrt(1.0 - jnp.exp(-2.0 * rate))
        down = iota((CHUNK, LANES), 0)
        along = iota((LANES, CHUNK), 1)
        entry = (scale.T * jnp.exp(-rate.T * (down + 1).astype(F32))).astype(BF16)
        leave = jnp.exp(-rate * (CHUNK - 1 - along).astype(F32))
        whole = jnp.exp(-rate * CHUNK)
        terms = scale * jnp.where(along == 0, 1.0, leave * jnp.exp(-rate))
        toeplitz = []
        for g in range(groups):
            line = jnp.sum(terms[g * modes : (g + 1) * modes], 0, keepdims=True)
            top = pltpu.roll(jnp.broadcast_to(line, (8, CHUNK)), 0, 1, stride=1, stride_axis=0)
            parts = [top] + [pltpu.roll(top, 8 * k, 1) for k in range(1, CHUNK // 8)]
            toeplitz.append(jnp.concatenate(parts, 0).astype(BF16))
        inside = group_mask(modes, size)
        state = left_state(states_ref, flags_ref, rate, lanes, modes, size, count) if carried else None
        taps = tap_rows(taps_ref, 0, lanes)
        skip = skip_ref[:, lanes]
        lane_group = iota((CHUNK, LANES), 1) // size
        for chunk in range(chunks):
            start = chunk * CHUNK
            mixed = mixed_ref[start : start + CHUNK, lanes]
            same = same_ref[chunk]
            left = [t * same for t in toeplitz]
            right = [jnp.where(lane_group == g, mixed, jnp.zeros_like(mixed)) for g in range(groups)]
            if state is not None:
                left.append(entry * keep_ref[chunk])
                right.append(state.astype(BF16))
            longer = jnp.dot(jnp.concatenate(left, 1), jnp.concatenate(right, 0), preferred_element_type=F32)
            if chunk + 1 < chunks:
                fresh = jnp.dot((leave * tail_ref[chunk]).astype(BF16), mixed, preferred_element_type=F32)
                held = flags_ref[2 + chunk] == 1
                fresh = jnp.where(inside, fresh, 0.0)
                state = fresh if state is None else jnp.where(held, whole * state, 0.0) + fresh
            body = longer + skip * mixed.astype(F32)
            for half in range(start, start + CHUNK, SPAN):
                gate = short_conv(extended(x_ref, halo_ref, 0, half, lanes), taps, lag_masks(mask_ref, half))
                inner = body[half - start : half - start + SPAN]
                summed = residual_ref[half : half + SPAN, lanes].astype(F32) + gate * inner
                if carried:
                    hand_over(out_ref, squares_ref, refs[5], summed, half, count // nblocks, lanes)
                else:
                    base_ref[half : half + SPAN, lanes] = summed
                    gate_ref[half : half + SPAN, lanes] = gate.astype(BF16)

    each_tile(width, tile)
    if carried:
        spare_ref[...] = out_ref[refs[5][nblocks], :, :width]


def add_kernel(
    modes, size, ndoc, nblocks,
    where_ref, lengths_ref, owner_ref,
    base_ref, gate_ref, rates_ref, residues_ref, states_ref,
    out_ref, spare_ref, squares_ref,
    keep_ref, flags_ref, slot_ref,
):
    count, width = base_ref.shape
    chunks = count // CHUNK

    @pl.when(pl.program_id(0) == 0)
    def _():
        where = where_ref[0]
        ends = running_ends(lengths_ref, ndoc)
        write_flags(flags_ref, ends, where, count, nblocks)
        write_slots(slot_ref, owner_ref, where, nblocks)
        squares_ref[...] = jnp.zeros_like(squares_ref)
        before = scalar_document(ends, where * count - 1)
        kept = jnp.int32(0)
        for end in reversed(ends):
            kept = jnp.where(end >= where * count, end - where * count, kept)
        kept = jnp.where(before < 0, 0, kept)
        keep_ref[...] = jnp.where(iota((count, LANES), 0) < kept, 1.0, 0.0).astype(F32)

    def tile(lanes):
        rate = tile_rates(rates_ref.at[0], lanes.start, size)
        scale = tile_rates(residues_ref.at[0], lanes.start, size) * jnp.sqrt(1.0 - jnp.exp(-2.0 * rate))
        down = iota((CHUNK, LANES), 0)
        entry = (scale.T * jnp.exp(-rate.T * (down + 1).astype(F32))).astype(BF16)
        whole = jnp.exp(-rate * CHUNK)
        state = left_state(states_ref, flags_ref, rate, lanes, modes, size, count)
        held = []
        for _ in range(chunks):
            held.append(state.astype(BF16))
            state = state * whole
        left = jnp.dot(entry, jnp.concatenate(held, 1), preferred_element_type=F32)
        for start in range(0, count, SPAN):
            low = start % CHUNK
            chunk = start // CHUNK
            carried = left[low : low + SPAN, chunk * LANES : (chunk + 1) * LANES] * keep_ref[start : start + SPAN, :]
            gate = gate_ref[start : start + SPAN, lanes].astype(F32)
            summed = base_ref[start : start + SPAN, lanes] + gate * carried
            hand_over(out_ref, squares_ref, slot_ref, summed, start, count // nblocks, lanes)

    each_tile(width, tile)
    spare_ref[...] = out_ref[slot_ref[nblocks], :, :width]


def norm_kernel(parts, where_ref, owner_ref, *refs):
    blocks = refs[:parts]
    spare_ref, gain_ref, out_ref = refs[parts:]
    nblocks, rows, _ = blocks[0].shape
    count, width = out_ref.shape
    spare_block = jnp.int32(0)
    for i in range(nblocks):
        spare_block = jnp.where(is_second(owner_ref, nblocks, i), i, spare_block)

    def block(i, carry):
        rows_out = pl.ds(pl.multiple_of(i * rows, rows), rows)
        is_spare = spare_block == i
        ahead = where_ref[0] - owner_ref[i]
        source = jnp.where(ahead < 0, ahead + nblocks, ahead)
        halves = jnp.where(is_spare, spare_ref[:, width:].astype(F32), blocks[-1][source, :, -LANES:].astype(F32))
        scale = halves[:, 0:1] + halves[:, 1:2]
        low = 0
        for part in range(parts):
            share = min(blocks[part].shape[2], width - low)
            for lane in range(0, share, LANES):
                outs = slice(low + lane, low + lane + LANES)
                value = blocks[part][source, :, lane : lane + LANES].astype(F32)
                value = jnp.where(is_spare, spare_ref[:, outs].astype(F32), value)
                out_ref[rows_out, outs] = (value * scale * gain_ref[:, outs]).astype(BF16)
            low += share
        return carry

    lax.fori_loop(0, nblocks, block, 0)


def params():
    return pltpu.CompilerParams(dimension_semantics=("arbitrary",), vmem_limit_bytes=VMEM_LIMIT)


def whole_array(rank):
    return lambda *_: (0,) * rank


def by_step(rates, wide, size):
    modes, groups = rates.shape
    held = wide // size
    return jnp.transpose(rates.reshape(modes, groups // held, held), (1, 0, 2))


def mix(scalars, x, halo, taps, rates, size, ndoc, copies):
    _, count, width = x.shape
    modes = rates.shape[0]
    wide = min(WIDE, width)
    deep = lambda t, *_: (0, 0, t)
    grid_spec = pltpu.PrefetchScalarGridSpec(
        num_scalar_prefetch=2,
        grid=(width // wide,),
        in_specs=[
            pl.BlockSpec((1, count, wide), lambda t, *_: (1, 0, t)),
            pl.BlockSpec((1, count, wide), lambda t, *_: (2, 0, t)),
            pl.BlockSpec((3, HALO, wide), deep),
            pl.BlockSpec((3, SHORT, wide), deep),
            pl.BlockSpec((1, modes, wide // size), lambda t, *_: (t, 0, 0)),
        ],
        out_specs=[
            pl.BlockSpec((count, wide), lambda t, *_: (0, t)),
            pl.BlockSpec((copies, modes, wide), deep),
        ],
        scratch_shapes=[pltpu.VMEM((3, count + 2 * HALO, LANES), F32), pltpu.VMEM((8, count), F32)],
    )
    return pl.pallas_call(
        functools.partial(mix_kernel, modes, size, ndoc),
        grid_spec=grid_spec,
        out_shape=[
            jax.ShapeDtypeStruct((count, width), BF16),
            jax.ShapeDtypeStruct((copies, modes, width), BF16),
        ],
        compiler_params=params(),
        cost_estimate=pl.CostEstimate(flops=60 * count * width, bytes_accessed=8 * count * width, transcendentals=count * width),
        name="mix",
    )(*scalars[:2], x, x, halo, taps, by_step(rates, wide, size))


def conv(low, share, room, scalars, x, halo, taps, mixed, rates, residues, skip, residual, states, size, ndoc, nblocks):
    _, count, width = x.shape
    modes = rates.shape[0]
    rows = count // nblocks
    wide = math.gcd(math.gcd(low, share), WIDE)
    first = low // wide
    carried = states is not None
    tile = lambda t, *_: (0, first + t)
    deep = lambda t, *_: (0, 0, first + t)
    step = pl.BlockSpec((1, modes, wide // size), lambda t, *_: (first + t, 0, 0))
    in_specs = [
        pl.BlockSpec((1, count, wide), deep),
        pl.BlockSpec((1, HALO, wide), deep),
        pl.BlockSpec((1, SHORT, wide), deep),
        pl.BlockSpec((count, wide), tile),
        step,
        step,
        pl.BlockSpec((1, wide), tile),
        pl.BlockSpec((count, wide), tile),
    ]
    operands = [x, halo, taps, mixed, by_step(rates, wide, size), by_step(residues, wide, size), skip, residual]
    scratch = [
        pltpu.VMEM((3, count + 2 * HALO, LANES), F32),
        pltpu.VMEM((count // CHUNK, CHUNK, CHUNK), BF16),
        pltpu.VMEM((count // CHUNK, CHUNK, LANES), BF16),
        pltpu.VMEM((count // CHUNK, LANES, CHUNK), F32),
        pltpu.SMEM((2 + count // CHUNK,), jnp.int32),
    ]
    if carried:
        in_specs.append(pl.BlockSpec((nblocks, modes, wide), deep))
        operands.append(states)
        scratch.append(pltpu.SMEM((nblocks + 1,), jnp.int32))
        out_specs, out_shape = handed(share, room, wide, count, nblocks)
    else:
        out_specs = [pl.BlockSpec((count, wide), lambda t, *_: (0, t))] * 2
        out_shape = [jax.ShapeDtypeStruct((count, share), F32), jax.ShapeDtypeStruct((count, share), BF16)]
    grid_spec = pltpu.PrefetchScalarGridSpec(
        num_scalar_prefetch=3, grid=(share // wide,), in_specs=in_specs, out_specs=out_specs, scratch_shapes=scratch
    )
    return pl.pallas_call(
        functools.partial(conv_kernel, modes, size, ndoc, nblocks, carried),
        grid_spec=grid_spec,
        out_shape=out_shape,
        compiler_params=params(),
        cost_estimate=pl.CostEstimate(
            flops=2 * 1152 * count * share, bytes_accessed=8 * count * share, transcendentals=count * share
        ),
        name="conv",
    )(*scalars, *operands)


def handed(share, room, wide, count, nblocks):
    rows = count // nblocks
    specs = [
        pl.BlockSpec((nblocks, rows, wide), lambda t, *_: (0, 0, t)),
        pl.BlockSpec((rows, wide), lambda t, *_: (0, t)),
        pl.BlockSpec((count, LANES), whole_array(2)),
    ]
    shapes = [
        jax.ShapeDtypeStruct((nblocks, rows, share + room), BF16),
        jax.ShapeDtypeStruct((rows, share), BF16),
        jax.ShapeDtypeStruct((count, LANES), F32),
    ]
    return specs, shapes


def add(scalars, base, gate, rates, residues, states, size, ndoc, nblocks):
    count, share = base.shape
    modes = rates.shape[0]
    wide = math.gcd(share, WIDE)
    tile = lambda t, *_: (0, t)
    step = pl.BlockSpec((1, modes, wide // size), lambda t, *_: (t, 0, 0))
    out_specs, out_shape = handed(share, 0, wide, count, nblocks)
    grid_spec = pltpu.PrefetchScalarGridSpec(
        num_scalar_prefetch=3,
        grid=(share // wide,),
        in_specs=[
            pl.BlockSpec((count, wide), tile),
            pl.BlockSpec((count, wide), tile),
            step,
            step,
            pl.BlockSpec((nblocks, modes, wide), lambda t, *_: (0, 0, t)),
        ],
        out_specs=out_specs,
        scratch_shapes=[
            pltpu.VMEM((count, LANES), F32),
            pltpu.SMEM((2 + count // CHUNK,), jnp.int32),
            pltpu.SMEM((nblocks + 1,), jnp.int32),
        ],
    )
    return pl.pallas_call(
        functools.partial(add_kernel, modes, size, ndoc, nblocks),
        grid_spec=grid_spec,
        out_shape=out_shape,
        compiler_params=params(),
        cost_estimate=pl.CostEstimate(flops=300 * count * share, bytes_accessed=8 * count * share, transcendentals=count * share),
        name="add",
    )(*scalars, base, gate, by_step(rates, wide, size), by_step(residues, wide, size), states)


def norm(where, owner, blocks, spare, gain):
    nblocks, rows, _ = blocks[0].shape
    count, width = nblocks * rows, gain.shape[1]
    vmem = pl.BlockSpec(memory_space=pltpu.VMEM)
    smem = pl.BlockSpec(memory_space=pltpu.SMEM)
    return pl.pallas_call(
        functools.partial(norm_kernel, len(blocks)),
        in_specs=[smem, smem] + [vmem] * (len(blocks) + 2),
        out_specs=vmem,
        out_shape=jax.ShapeDtypeStruct((count, width), BF16),
        compiler_params=pltpu.CompilerParams(vmem_limit_bytes=16 * 1024 * 1024),
        cost_estimate=pl.CostEstimate(flops=3 * count * width, bytes_accessed=4 * count * width, transcendentals=0),
        name="norm",
    )(where, owner, *blocks, spare, gain)


def on_device(features, residual, short_taps, rates, residues, skip, gain, lengths, owner):
    count, _, width = features.shape
    size = width // rates.shape[0]
    ndoc = lengths.shape[0]
    nblocks = lax.axis_size("ctx")
    rows = count // nblocks
    where = lax.axis_index("ctx")
    x = jnp.transpose(features, (1, 0, 2))
    pairs = [(i, i + 1) for i in range(nblocks - 1)]
    halo = lax.ppermute(x[:, count - HALO :], "ctx", pairs)

    scalars = (where.reshape(1).astype(jnp.int32), lengths, owner)
    rates, residues = rates.T, residues.T

    table = owner.reshape(nblocks, nblocks)
    ids = jnp.arange(nblocks, dtype=jnp.int32)
    mine = lax.dynamic_index_in_dim(table, where, 0, keepdims=False)
    twice = jnp.any((mine[:, None] == mine[None, :]) & (ids[None, :] < ids[:, None]), 1)
    unused = nblocks * (nblocks - 1) // 2 - jnp.sum(jnp.where(twice, 0, mine))
    slots = jnp.where(twice, unused, mine).astype(jnp.int32)
    spare_shift = jnp.sum(jnp.where(twice, table[0], 0))

    def exchanged(value):
        return lax.all_to_all(value, "ctx", split_axis=0, concat_axis=0, tiled=True)

    first = width * SPLIT[0] // sum(SPLIT)
    second = width - first
    mixed, copies = mix(scalars, x, halo, short_taps, rates, size, ndoc, nblocks)
    states = exchanged(copies)
    shared = (scalars, x, halo, short_taps, mixed, rates, residues, skip.reshape(1, width), residual)
    base, gate = conv(0, first, 0, *shared, None, size, ndoc, nblocks)
    out, spare, squares = add(scalars, base, gate, rates, residues, states, size, ndoc, nblocks)
    block = exchanged(out)
    out, last_spare, last_squares = conv(first, second, LANES, *shared, states, size, ndoc, nblocks)
    mean = lax.psum(jnp.sum(squares + last_squares, 1), "mp") / (width * lax.axis_size("mp"))
    inverse = lax.rsqrt(mean + EPS)
    high = lax.reduce_precision(inverse, 8, 7)
    column = iota((count, LANES), 1)
    halves = jnp.where(column == 0, high[:, None], jnp.where(column == 1, (inverse - high)[:, None], 0.0))
    halves = halves.reshape(nblocks, rows, LANES)
    in_slot = slots[None, :] == ids[:, None]
    by_slot = jnp.sum(jnp.where(in_slot[:, :, None, None], halves[None], 0.0), 1).astype(BF16)
    spare_halves = jnp.sum(jnp.where(twice[:, None, None], halves, 0.0), 0).astype(BF16)
    out = lax.dynamic_update_slice(out, by_slot, (0, 0, second))
    out, block = lax.optimization_barrier((out, block))
    blocks = [block, exchanged(out)]
    spares = jnp.concatenate([spare, last_spare, spare_halves], 1)

    def moved(by):
        return lambda value: lax.ppermute(value, "ctx", [(s, (s + by) % nblocks) for s in range(nblocks)])

    spare = lax.switch(spare_shift, [lambda value: value] + [moved(d) for d in range(1, nblocks)], spares)
    return norm(scalars[0], owner, blocks, spare, gain.reshape(1, width))


def solution(mesh):
    return jax.shard_map(
        on_device,
        mesh=mesh,
        in_specs=(
            P("ctx", None, "mp"),
            P("ctx", "mp"),
            P(None, None, "mp"),
            P("mp", None),
            P("mp", None),
            P("mp"),
            P("mp"),
            P(),
            P(),
        ),
        out_specs=P("ctx", "mp"),
        check_vma=False,
    )
```

profile of v0, /device:TPU:14, one launch (start us, length us, event | category | flops | bytes accessed | tf_op | source)
XLA Modules:
  0.0 120.6 jit_solution(14648771845349253297)
XLA Ops:
  0.0 0.9 slice.9
  0.9 3.4 %collective-permute-start.7 = (bf16[3,8,2048]{2,1,0:T(8,128)(2,1)S(1)}, bf16[3,8,2048]{2,1,0:T(8,128)(2,1)S(1)}, u32[]{:S(2)}, u32[]{:S(2)}) collective-permute-start(bf16[3,8,2048]{2,1,0:T(8,128)(2,1)S(1)} %slice.9), channel_id=1, source_target_pairs={{0,4},{4,8},{8,12},{12,16},{16,20},{20,24},{24,28},{1,5},{5,9},{9,... | collective-permute-start | bytes 294920 | tf_op jit(solution)/shard_map/ppermute | solution.py:541
  4.3 0.8 reshape.95
  5.1 0.6 copy.19
  5.7 1.7 %collective-permute-done.7.halo_ref.refs_1_ = bf16[3,8,2048]{2,1,0:T(8,128)(2,1)S(1)} collective-permute-done((bf16[3,8,2048]{2,1,0:T(8,128)(2,1)S(1)}, bf16[3,8,2048]{2,1,0:T(8,128)(2,1)S(1)}, u32[]{:S(2)}, u32[]{:S(2)}) %collective-permute-start.7) | collective-permute-done | bytes 98336 | tf_op jit(solution)/shard_map/ppermute | solution.py:541
  7.4 0.6 copy-done.4
  8.1 13.4 %mix.1 = (bf16[512,2048]{1,0:T(8,128)(2,1)}, bf16[8,16,2048]{2,1,0:T(8,128)(2,1)}) custom-call(s32[1]{0:T(128)} %bitcast.where_ref, s32[8]{0:T(128)} %lengths_ref.7, bf16[3,512,2048]{2,1,0:T(8,128)(2,1)} %bitcast.25, bf16[3,512,2048]{2,1,0:T(8,128)(2,1)} %bitcast.26, bf16[3,8,2048]{2,1,0:T(8,128)(2,1)} %copy-done.4, f32[3,7,2048]{2,1,0:T(8,128)} %refs_2_.3, ...), custom_call_target="tpu_custom_call" | custom-call | flops 62914560 | bytes 8388608 | tf_op jit(solution)/shard_map/mix/pallas_call | solution.py:403
  21.5 6.2 %all-to-all-start = ((bf16[8,16,2048]{2,1,0:T(8,128)(2,1)}), bf16[8,16,2048]{2,1,0:T(8,128)(2,1)S(1)}, u32[]{:S(2)}, u32[]{:S(2)}) async-start(bf16[8,16,2048]{2,1,0:T(8,128)(2,1)} %get-tuple-element.35), calls=%async_computation | async-start | bytes 1048576 | tf_op jit(solution)/shard_map/all_to_all | solution.py:555
  28.1 0.7 select_reduce_fusion.2
  29.4 0.7 copy_bitcast_fusion
  30.0 8.3 %conv.3 = (f32[512,768]{1,0:T(8,128)}, bf16[512,768]{1,0:T(8,128)(2,1)}) custom-call(s32[1]{0:T(128)} %bitcast.where_ref, s32[8]{0:T(128)} %lengths_ref.7, s32[64]{0:T(128)} %owner_ref.7, bf16[3,512,2048]{2,1,0:T(8,128)(2,1)} %bitcast.27, bf16[3,8,2048]{2,1,0:T(8,128)(2,1)} %copy-done.4, f32[3,7,2048]{2,1,0:T(8,128)} %refs_2_.3, ...), custom_call_target="tpu_custom_call" | custom-call | flops 905969664 | bytes 3145728 | tf_op jit(solution)/shard_map/conv/pallas_call | solution.py:455
  38.3 0.8 copy-done.3
  39.1 5.7 %add.32 = (bf16[8,64,768]{2,1,0:T(8,128)(2,1)}, bf16[64,768]{1,0:T(8,128)(2,1)}, f32[512,128]{1,0:T(8,128)}) custom-call(s32[1]{0:T(128)} %bitcast.where_ref, s32[8]{0:T(128)} %lengths_ref.7, s32[64]{0:T(128)} %owner_ref.7, f32[512,768]{1,0:T(8,128)} %get-tuple-element.37.base_ref, bf16[512,768]{1,0:T(8,128)(2,1)} %get-tuple-element.38.gate_ref, ...), custom_call_target="tpu_custom_call" | custom-call | flops 117964800 | bytes 3145728 | tf_op jit(solution)/shard_map/add/pallas_call | solution.py:506
  44.8 6.2 %all-to-all-start.1 = ((bf16[8,64,768]{2,1,0:T(8,128)(2,1)}), bf16[8,64,768]{2,1,0:T(8,128)(2,1)S(1)}, u32[]{:S(2)}, u32[]{:S(2)}) async-start(bf16[8,64,768]{2,1,0:T(8,128)(2,1)} %get-tuple-element.41), calls=%async_computation.1 | async-start | bytes 1572864 | tf_op jit(solution)/shard_map/all_to_all | solution.py:555
  51.1 13.5 %conv.2 = (bf16[8,64,1408]{2,1,0:T(8,128)(2,1)}, bf16[64,1280]{1,0:T(8,128)(2,1)}, f32[512,128]{1,0:T(8,128)}) custom-call(s32[1]{0:T(128)} %bitcast.where_ref, s32[8]{0:T(128)} %lengths_ref.7, s32[64]{0:T(128)} %owner_ref.7, bf16[3,512,2048]{2,1,0:T(8,128)(2,1)} %bitcast.28, bf16[3,8,2048]{2,1,0:T(8,128)(2,1)} %copy-done.4, f32[3,7,2048]{2,1,0:T(8,128)} %refs_2_.3, ...), custom_call_target="tpu_custom_call" | custom-call | flops 1509949440 | bytes 5242880 | tf_op jit(solution)/shard_map/conv/pallas_call | solution.py:455
  64.6 1.1 add_reduce_fusion
  65.7 5.9 %psum.7 = f32[512]{0:T(512)S(1)} all-reduce(f32[512]{0:T(512)S(1)} %add_reduce_fusion), channel_id=1, replica_groups=mesh['ctx'=8,'mp'=4] {'mp'}, use_global_device_ids=true, to_apply=%region_3.4 | all-reduce | flops 512 | bytes 4096 | tf_op jit(solution)/shard_map/psum | solution.py:566
  72.0 0.2 select_reduce_fusion
  72.3 0.7 convert_dynamic-update-slice_fusion
  73.0 5.6 %all-to-all-start.2 = ((bf16[8,64,1408]{2,1,0:T(8,128)(2,1)}), bf16[8,64,1408]{2,1,0:T(8,128)(2,1)S(1)}, u32[]{:S(2)}, u32[]{:S(2)}) async-start(bf16[8,64,1408]{2,1,0:T(8,128)(2,1)} %convert_dynamic-update-slice_fusion), calls=%async_computation.2 | async-start | bytes 2883584 | tf_op jit(solution)/shard_map/all_to_all | solution.py:555
  79.3 37.8 %conditional.1 = (bf16[64,2176]{1,0:T(8,128)(2,1)S(1)}) conditional(s32[]{:T(128)} %clamp.3, bf16[64,2176]{1,0:T(8,128)(2,1)S(1)} %pad_maximum_fusion, bf16[64,2176]{1,0:T(8,128)(2,1)S(1)} %pad_maximum_fusion, bf16[64,2176]{1,0:T(8,128)(2,1)S(1)} %pad_maximum_fusion, ...), branch_computations={%region_7.8_spmd, %region_8.9_spmd, %region_9.10_spmd, %region_10.... | conditional | bytes 1671216 | solution.py:583
  79.3 0.6 collective-permute-start.6
  79.9 37.1 %collective-permute-done.6 = bf16[64,2176]{1,0:T(8,128)(2,1)S(1)} collective-permute-done((bf16[64,2176]{1,0:T(8,128)(2,1)S(1)}, bf16[64,2176]{1,0:T(8,128)(2,1)S(1)}, u32[]{:S(2)}, u32[]{:S(2)}) %collective-permute-start.6) | collective-permute-done | bytes 278560 | tf_op jit(solution)/shard_map/cond/branch_7_fun/ppermute | solution.py:581
  117.1 3.5 %norm.1 = bf16[512,2048]{1,0:T(8,128)(2,1)} custom-call(s32[1]{0:T(128)} %bitcast.where_ref, s32[64]{0:T(128)S(1)} %copy-done.1, bf16[8,64,768]{2,1,0:T(8,128)(2,1)S(1)} %all-to-all-done.1.refs_0_, bf16[8,64,1408]{2,1,0:T(8,128)(2,1)S(1)} %all-to-all-done.2.refs_1_, bf16[64,2176]{1,0:T(8,128)(2,1)S(1)} %get-tuple-element.56.refs_2_, f32[1,2048]{1,0:T(1,128)S(1)} %bitcast.23), custom_call_target="tpu_custom_call" | custom-call | flops 3145728 | bytes 4194304 | tf_op jit(solution)/shard_map/norm/pallas_call | solution.py:521
  (35 shorter events, 0.9 us)
Async XLA Ops:
  0.9 6.5 %collective-permute-start.7 = (bf16[3,8,2048]{2,1,0:T(8,128)(2,1)S(1)}, bf16[3,8,2048]{2,1,0:T(8,128)(2,1)S(1)}, u32[]{:S(2)}, u32[]{:S(2)}) collective-permute-start(bf16[3,8,2048]{2,1,0:T(8,128)(2,1)S(1)} %slice.9), channel_id=1, source_target_pairs={{0,4},{4,8},{8,12},{12,16},{16,20},{20,24},{24,28},{1,5},{5,9},{9,... | collective-permute-start | bytes 294920 | tf_op jit(solution)/shard_map/ppermute | solution.py:541
  7.4 0.6 copy-start.4
  8.0 19.6 %copy-start.8 = (f32[128,16]{0,1:T(8,128)S(1)}, f32[128,16]{0,1:T(8,128)}, u32[]{:S(2)}) copy-start(f32[128,16]{0,1:T(8,128)} %param.20) | copy-start | bytes 24580
  8.0 19.7 %copy-start.9 = (f32[128,16]{0,1:T(8,128)S(1)}, f32[128,16]{0,1:T(8,128)}, u32[]{:S(2)}) copy-start(f32[128,16]{0,1:T(8,128)} %param.21) | copy-start | bytes 24580
  8.0 19.8 %copy-start = (s32[64]{0:T(128)S(1)}, s32[64]{0:T(128)}, u32[]{:S(2)}) copy-start(s32[64]{0:T(128)} %owner_ref.7) | copy-start | bytes 772
  21.5 16.9 %all-to-all-start = ((bf16[8,16,2048]{2,1,0:T(8,128)(2,1)}), bf16[8,16,2048]{2,1,0:T(8,128)(2,1)S(1)}, u32[]{:S(2)}, u32[]{:S(2)}) async-start(bf16[8,16,2048]{2,1,0:T(8,128)(2,1)} %get-tuple-element.35), calls=%async_computation | async-start | bytes 1048576 | tf_op jit(solution)/shard_map/all_to_all | solution.py:555
  38.3 0.8 copy-start.3
  44.8 28.2 %all-to-all-start.1 = ((bf16[8,64,768]{2,1,0:T(8,128)(2,1)}), bf16[8,64,768]{2,1,0:T(8,128)(2,1)S(1)}, u32[]{:S(2)}, u32[]{:S(2)}) async-start(bf16[8,64,768]{2,1,0:T(8,128)(2,1)} %get-tuple-element.41), calls=%async_computation.1 | async-start | bytes 1572864 | tf_op jit(solution)/shard_map/all_to_all | solution.py:555
  51.1 13.5 %copy-start.5 = (f32[512,128]{1,0:T(8,128)S(1)}, f32[512,128]{1,0:T(8,128)}, u32[]{:S(2)}) copy-start(f32[512,128]{1,0:T(8,128)} %get-tuple-element.39) | copy-start | bytes 786436
  64.6 14.6 %copy-start.6 = (bf16[64,1280]{1,0:T(8,128)(2,1)S(1)}, bf16[64,1280]{1,0:T(8,128)(2,1)}, u32[]{:S(2)}) copy-start(bf16[64,1280]{1,0:T(8,128)(2,1)} %get-tuple-element.45) | copy-start | bytes 491524
  64.6 14.6 %copy-start.7 = (bf16[64,768]{1,0:T(8,128)(2,1)S(1)}, bf16[64,768]{1,0:T(8,128)(2,1)}, u32[]{:S(2)}) copy-start(bf16[64,768]{1,0:T(8,128)(2,1)} %get-tuple-element.44) | copy-start | bytes 294916
  73.0 44.1 %all-to-all-start.2 = ((bf16[8,64,1408]{2,1,0:T(8,128)(2,1)}), bf16[8,64,1408]{2,1,0:T(8,128)(2,1)S(1)}, u32[]{:S(2)}, u32[]{:S(2)}) async-start(bf16[8,64,1408]{2,1,0:T(8,128)(2,1)} %convert_dynamic-update-slice_fusion), calls=%async_computation.2 | async-start | bytes 2883584 | tf_op jit(solution)/shard_map/all_to_all | solution.py:555
  79.2 37.9 %copy-start.1 = (s32[64]{0:T(128)S(1)}, s32[64]{0:T(128)}, u32[]{:S(2)}) copy-start(s32[64]{0:T(128)} %owner_ref.7) | copy-start | bytes 772
  79.2 37.9 %copy-start.2 = (f32[2048]{0:T(1024)S(1)}, f32[2048]{0:T(1024)}, u32[]{:S(2)}) copy-start(f32[2048]{0:T(1024)} %param.23) | copy-start | bytes 24580
  79.3 37.7 %collective-permute-start.6 = (bf16[64,2176]{1,0:T(8,128)(2,1)S(1)}, bf16[64,2176]{1,0:T(8,128)(2,1)S(1)}, u32[]{:S(2)}, u32[]{:S(2)}) collective-permute-start(bf16[64,2176]{1,0:T(8,128)(2,1)S(1)} %param.7), channel_id=1, source_target_pairs={{0,28},{4,0},{8,4},{12,8},{16,12},{20,16},{24,20},{28,24},{1,29},{... | collective-permute-start | bytes 835592 | tf_op jit(solution)/shard_map/cond/branch_7_fun/ppermute | solution.py:581
where the time goes:
time: 122 us; the launch traced here: 121 us
  Pallas kernels  44.4 us (36%)
  waiting for transfers between devices  38.8 us (32%)
  starting transfers between devices  22 us (18%)
  blocking collectives  5.91 us (5%)
  local copies, waits for them, and re-layouts  5.55 us (5%)
  other arithmetic  2.5 us (2%)
  between operations  1.4 us (1%)
    ppermute x1, waiting for transfers between devices, moved(): lax.ppermute(value, 'ctx', [(s, (s + by) % nblocks) for s in range(nblock...  37.1 us
    pallas_call x2, Pallas kernels, conv(): pl.pallas_call(functools.partial(conv_kernel, modes, size, ndoc, nblocks,...  21.8 us
    all_to_all x3, starting transfers between devices, exchanged(): return lax.all_to_all(value, 'ctx', split_axis=0, concat_axis=0, tiled=True)  18 us
    pallas_call x1, Pallas kernels, mix(): pl.pallas_call(functools.partial(mix_kernel, modes, size, ndoc), grid_spe...  13.4 us
    psum x1, blocking collectives, on_device(): lax.psum(jnp.sum(squares + last_squares, 1), 'mp')  5.91 us
    pallas_call x1, Pallas kernels, add(): pl.pallas_call(functools.partial(add_kernel, modes, size, ndoc, nblocks),...  5.67 us
    pallas_call x1, Pallas kernels, norm(): pl.pallas_call(functools.partial(norm_kernel, len(blocks)), in_specs=[sme...  3.51 us
    ppermute x1, starting transfers between devices, on_device(): halo = lax.ppermute(x[:, count - HALO:], 'ctx', pairs)  3.42 us
  transfers between devices with their start and end apart: 5, of which 2 were waited for; matrix products, arithmetic and copies ran while one was open for 5% of the time, Pallas kernels for 18%

commit v1 on v0

--- a/solution.py
+++ b/solution.py
@@ -13,7 +13,7 @@
 CHUNK = 128
 HALO = 8
 EPS = 1e-06
-SPLIT = (3, 5)
+SPLIT = (4, 4)
 WIDE = 512
 SPAN = 64
 F32 = jnp.float32
@@ -573,7 +573,6 @@
     by_slot = jnp.sum(jnp.where(in_slot[:, :, None, None], halves[None], 0.0), 1).astype(BF16)
     spare_halves = jnp.sum(jnp.where(twice[:, None, None], halves, 0.0), 0).astype(BF16)
     out = lax.dynamic_update_slice(out, by_slot, (0, 0, second))
-    out, block = lax.optimization_barrier((out, block))
     blocks = [block, exchanged(out)]
     spares = jnp.concatenate([spare, last_spare, spare_halves], 1)
 

time: 122 us -> 121 us (level)
  the two profiles are of different devices: /device:TPU:14 before, /device:TPU:8 now
where the time goes in v1:
time: 121 us
  Pallas kernels  43.7 us (36%)
  waiting for transfers between devices  38.7 us (32%)
  starting transfers between devices  23.1 us (19%)
  blocking collectives  5.96 us (5%)
  local copies, waits for them, and re-layouts  5.39 us (4%)
  other arithmetic  2.57 us (2%)
  between operations  1.49 us (1%)
    ppermute x1, waiting for transfers between devices, moved(): lax.ppermute(value, 'ctx', [(s, (s + by) % nblocks) for s in range(nblock...  33.2 us
    pallas_call x2, Pallas kernels, conv(): pl.pallas_call(functools.partial(conv_kernel, modes, size, ndoc, nblocks,...  20.9 us
    all_to_all x3, starting transfers between devices, exchanged(): return lax.all_to_all(value, 'ctx', split_axis=0, concat_axis=0, tiled=True)  16.4 us
    pallas_call x1, Pallas kernels, mix(): pl.pallas_call(functools.partial(mix_kernel, modes, size, ndoc), grid_spe...  13.4 us
    psum x1, blocking collectives, on_device(): lax.psum(jnp.sum(squares + last_squares, 1), 'mp')  5.96 us
    pallas_call x1, Pallas kernels, add(): pl.pallas_call(functools.partial(add_kernel, modes, size, ndoc, nblocks),...  5.84 us
    pallas_call x1, Pallas kernels, norm(): pl.pallas_call(functools.partial(norm_kernel, len(blocks)), in_specs=[sme...  3.52 us
    ppermute x1, starting transfers between devices, on_device(): halo = lax.ppermute(x[:, count - HALO:], 'ctx', pairs)  3.42 us
  transfers between devices with their start and end apart: 5, of which 4 were waited for; matrix products, arithmetic and copies ran while one was open for 5% of the time, Pallas kernels for 17%

profile of v1, /device:TPU:8, one launch (start us, length us, event | category | flops | bytes accessed | tf_op | source)
XLA Modules:
  0.0 121.0 jit_solution(18398996771635446591)
XLA Ops:
  0.0 0.9 slice.9
  0.9 3.4 %collective-permute-start.7 = (bf16[3,8,2048]{2,1,0:T(8,128)(2,1)S(1)}, bf16[3,8,2048]{2,1,0:T(8,128)(2,1)S(1)}, u32[]{:S(2)}, u32[]{:S(2)}) collective-permute-start(bf16[3,8,2048]{2,1,0:T(8,128)(2,1)S(1)} %slice.9), channel_id=1, source_target_pairs={{0,4},{4,8},{8,12},{12,16},{16,20},{20,24},{24,28},{1,5},{5,9},{9,... | collective-permute-start | bytes 294920 | tf_op jit(solution)/shard_map/ppermute | solution.py:541
  4.3 0.8 reshape.93
  5.7 2.6 %collective-permute-done.7.halo_ref.refs_1_ = bf16[3,8,2048]{2,1,0:T(8,128)(2,1)S(1)} collective-permute-done((bf16[3,8,2048]{2,1,0:T(8,128)(2,1)S(1)}, bf16[3,8,2048]{2,1,0:T(8,128)(2,1)S(1)}, u32[]{:S(2)}, u32[]{:S(2)}) %collective-permute-start.7) | collective-permute-done | bytes 98336 | tf_op jit(solution)/shard_map/ppermute | solution.py:541
  8.3 0.6 copy-done.5
  8.9 13.4 %mix.1 = (bf16[512,2048]{1,0:T(8,128)(2,1)}, bf16[8,16,2048]{2,1,0:T(8,128)(2,1)}) custom-call(s32[1]{0:T(128)} %bitcast.where_ref, s32[8]{0:T(128)} %lengths_ref.7, bf16[3,512,2048]{2,1,0:T(8,128)(2,1)} %bitcast.24, bf16[3,512,2048]{2,1,0:T(8,128)(2,1)} %bitcast.25, bf16[3,8,2048]{2,1,0:T(8,128)(2,1)} %copy-done.5, f32[3,7,2048]{2,1,0:T(8,128)} %refs_2_.3, ...), custom_call_target="tpu_custom_call" | custom-call | flops 62914560 | bytes 8388608 | tf_op jit(solution)/shard_map/mix/pallas_call | solution.py:403
  22.4 5.4 %all-to-all-start = ((bf16[8,16,2048]{2,1,0:T(8,128)(2,1)}), bf16[8,16,2048]{2,1,0:T(8,128)(2,1)S(1)}, u32[]{:S(2)}, u32[]{:S(2)}) async-start(bf16[8,16,2048]{2,1,0:T(8,128)(2,1)} %get-tuple-element.35), calls=%async_computation | async-start | bytes 1048576 | tf_op jit(solution)/shard_map/all_to_all | solution.py:555
  27.8 0.6 copy.16
  28.5 10.0 %conv.2 = (f32[512,1024]{1,0:T(8,128)}, bf16[512,1024]{1,0:T(8,128)(2,1)}) custom-call(s32[1]{0:T(128)} %bitcast.where_ref, s32[8]{0:T(128)} %lengths_ref.7, s32[64]{0:T(128)} %owner_ref.7, bf16[3,512,2048]{2,1,0:T(8,128)(2,1)} %bitcast.26, bf16[3,8,2048]{2,1,0:T(8,128)(2,1)} %copy-done.5, f32[3,7,2048]{2,1,0:T(8,128)} %refs_2_.3, ...), custom_call_target="tpu_custom_call" | custom-call | flops 1207959552 | bytes 4194304 | tf_op jit(solution)/shard_map/conv/pallas_call | solution.py:455
  38.5 1.3 %all-to-all-done.states_ref.refs_8_ = bf16[8,16,2048]{2,1,0:T(8,128)(2,1)S(1)} async-done(((bf16[8,16,2048]{2,1,0:T(8,128)(2,1)}), bf16[8,16,2048]{2,1,0:T(8,128)(2,1)S(1)}, u32[]{:S(2)}, u32[]{:S(2)}) %all-to-all-start) | async-done | bytes 524320 | tf_op jit(solution)/shard_map/all_to_all | solution.py:555
  39.8 0.8 copy-done.4
  40.6 5.8 %add.32 = (bf16[8,64,1024]{2,1,0:T(8,128)(2,1)}, bf16[64,1024]{1,0:T(8,128)(2,1)}, f32[512,128]{1,0:T(8,128)}) custom-call(s32[1]{0:T(128)} %bitcast.where_ref, s32[8]{0:T(128)} %lengths_ref.7, s32[64]{0:T(128)} %owner_ref.7, f32[512,1024]{1,0:T(8,128)} %get-tuple-element.33.base_ref, bf16[512,1024]{1,0:T(8,128)(2,1)} %get-tuple-element.34.gate_ref, ...), custom_call_target="tpu_custom_call" | custom-call | flops 157286400 | bytes 4194304 | tf_op jit(solution)/shard_map/add/pallas_call | solution.py:506
  46.4 4.9 %all-to-all-start.1 = ((bf16[8,64,1024]{2,1,0:T(8,128)(2,1)}), bf16[8,64,1024]{2,1,0:T(8,128)(2,1)S(1)}, u32[]{:S(2)}, u32[]{:S(2)}) async-start(bf16[8,64,1024]{2,1,0:T(8,128)(2,1)} %get-tuple-element.36), calls=%async_computation.1 | async-start | bytes 2097152 | tf_op jit(solution)/shard_map/all_to_all | solution.py:555
  51.6 0.7 select_reduce_fusion.2
  53.1 10.9 %conv.3 = (bf16[8,64,1152]{2,1,0:T(8,128)(2,1)}, bf16[64,1024]{1,0:T(8,128)(2,1)}, f32[512,128]{1,0:T(8,128)}) custom-call(s32[1]{0:T(128)} %bitcast.where_ref, s32[8]{0:T(128)} %lengths_ref.7, s32[64]{0:T(128)} %owner_ref.7, bf16[3,512,2048]{2,1,0:T(8,128)(2,1)} %bitcast.27, bf16[3,8,2048]{2,1,0:T(8,128)(2,1)} %copy-done.5, f32[3,7,2048]{2,1,0:T(8,128)} %refs_2_.3, ...), custom_call_target="tpu_custom_call" | custom-call | flops 1207959552 | bytes 4194304 | tf_op jit(solution)/shard_map/conv/pallas_call | solution.py:455
  64.0 1.1 add_reduce_fusion
  65.2 6.0 %psum.7 = f32[512]{0:T(512)S(1)} all-reduce(f32[512]{0:T(512)S(1)} %add_reduce_fusion), channel_id=1, replica_groups=mesh['ctx'=8,'mp'=4] {'mp'}, use_global_device_ids=true, to_apply=%region_3.4 | all-reduce | flops 512 | bytes 4096 | tf_op jit(solution)/shard_map/psum | solution.py:566
  71.8 0.7 convert_dynamic-update-slice_fusion
  72.5 1.6 %all-to-all-done.1.refs_0_ = bf16[8,64,1024]{2,1,0:T(8,128)(2,1)S(1)} async-done(((bf16[8,64,1024]{2,1,0:T(8,128)(2,1)}), bf16[8,64,1024]{2,1,0:T(8,128)(2,1)S(1)}, u32[]{:S(2)}, u32[]{:S(2)}) %all-to-all-start.1) | async-done | bytes 1048608 | tf_op jit(solution)/shard_map/all_to_all | solution.py:555
  74.1 6.0 %all-to-all-start.2 = ((bf16[8,64,1152]{2,1,0:T(8,128)(2,1)}), bf16[8,64,1152]{2,1,0:T(8,128)(2,1)S(1)}, u32[]{:S(2)}, u32[]{:S(2)}) async-start(bf16[8,64,1152]{2,1,0:T(8,128)(2,1)} %convert_dynamic-update-slice_fusion), calls=%async_computation.2 | async-start | bytes 2359296 | tf_op jit(solution)/shard_map/all_to_all | solution.py:555
  80.8 36.6 %conditional.1 = (bf16[64,2176]{1,0:T(8,128)(2,1)S(1)}) conditional(s32[]{:T(128)} %clamp.3, bf16[64,2176]{1,0:T(8,128)(2,1)S(1)} %pad_maximum_fusion, bf16[64,2176]{1,0:T(8,128)(2,1)S(1)} %pad_maximum_fusion, bf16[64,2176]{1,0:T(8,128)(2,1)S(1)} %pad_maximum_fusion, ...), branch_computations={%region_7.8_spmd, %region_8.9_spmd, %region_9.10_spmd, %region_10.... | conditional | bytes 1671216 | solution.py:582
  80.8 3.3 %collective-permute-start.4 = (bf16[64,2176]{1,0:T(8,128)(2,1)S(1)}, bf16[64,2176]{1,0:T(8,128)(2,1)S(1)}, u32[]{:S(2)}, u32[]{:S(2)}) collective-permute-start(bf16[64,2176]{1,0:T(8,128)(2,1)S(1)} %param.5), channel_id=1, source_target_pairs={{0,20},{4,24},{8,28},{12,0},{16,4},{20,8},{24,12},{28,16},{1,21},{... | collective-permute-start | bytes 835592 | tf_op jit(solution)/shard_map/cond/branch_5_fun/ppermute | solution.py:580
  84.2 33.2 %collective-permute-done.4 = bf16[64,2176]{1,0:T(8,128)(2,1)S(1)} collective-permute-done((bf16[64,2176]{1,0:T(8,128)(2,1)S(1)}, bf16[64,2176]{1,0:T(8,128)(2,1)S(1)}, u32[]{:S(2)}, u32[]{:S(2)}) %collective-permute-start.4) | collective-permute-done | bytes 278560 | tf_op jit(solution)/shard_map/cond/branch_5_fun/ppermute | solution.py:580
  117.4 3.5 %norm.1 = bf16[512,2048]{1,0:T(8,128)(2,1)} custom-call(s32[1]{0:T(128)} %bitcast.where_ref, s32[64]{0:T(128)S(1)} %copy-done.2, bf16[8,64,1024]{2,1,0:T(8,128)(2,1)S(1)} %all-to-all-done.1.refs_0_, bf16[8,64,1152]{2,1,0:T(8,128)(2,1)S(1)} %all-to-all-done.2.refs_1_, bf16[64,2176]{1,0:T(8,128)(2,1)S(1)} %get-tuple-element.50.refs_2_, f32[1,2048]{1,0:T(1,128)S(1)} %bitcast.22), custom_call_target="tpu_custom_call" | custom-call | flops 3145728 | bytes 4194304 | tf_op jit(solution)/shard_map/norm/pallas_call | solution.py:521
  (34 shorter events, 1.7 us)
Async XLA Ops:
  0.9 7.4 %collective-permute-start.7 = (bf16[3,8,2048]{2,1,0:T(8,128)(2,1)S(1)}, bf16[3,8,2048]{2,1,0:T(8,128)(2,1)S(1)}, u32[]{:S(2)}, u32[]{:S(2)}) collective-permute-start(bf16[3,8,2048]{2,1,0:T(8,128)(2,1)S(1)} %slice.9), channel_id=1, source_target_pairs={{0,4},{4,8},{8,12},{12,16},{16,20},{20,24},{24,28},{1,5},{5,9},{9,... | collective-permute-start | bytes 294920 | tf_op jit(solution)/shard_map/ppermute | solution.py:541
  8.3 0.6 copy-start.5
  8.9 18.8 %copy-start.9 = (f32[128,16]{0,1:T(8,128)S(1)}, f32[128,16]{0,1:T(8,128)}, u32[]{:S(2)}) copy-start(f32[128,16]{0,1:T(8,128)} %param.21) | copy-start | bytes 24580
  8.9 19.5 %copy-start = (s32[64]{0:T(128)S(1)}, s32[64]{0:T(128)}, u32[]{:S(2)}) copy-start(s32[64]{0:T(128)} %owner_ref.7) | copy-start | bytes 772
  22.4 17.5 %all-to-all-start = ((bf16[8,16,2048]{2,1,0:T(8,128)(2,1)}), bf16[8,16,2048]{2,1,0:T(8,128)(2,1)S(1)}, u32[]{:S(2)}, u32[]{:S(2)}) async-start(bf16[8,16,2048]{2,1,0:T(8,128)(2,1)} %get-tuple-element.35), calls=%async_computation | async-start | bytes 1048576 | tf_op jit(solution)/shard_map/all_to_all | solution.py:555
  39.8 0.8 copy-start.4
  40.6 11.0 %copy-start.1 = (s32[64]{0:T(128)S(1)}, s32[64]{0:T(128)}, u32[]{:S(2)}) copy-start(s32[64]{0:T(128)} %owner_ref.7) | copy-start | bytes 772
  46.4 27.6 %all-to-all-start.1 = ((bf16[8,64,1024]{2,1,0:T(8,128)(2,1)}), bf16[8,64,1024]{2,1,0:T(8,128)(2,1)S(1)}, u32[]{:S(2)}, u32[]{:S(2)}) async-start(bf16[8,64,1024]{2,1,0:T(8,128)(2,1)} %get-tuple-element.36), calls=%async_computation.1 | async-start | bytes 2097152 | tf_op jit(solution)/shard_map/all_to_all | solution.py:555
  53.0 11.0 %copy-start.6 = (f32[512,128]{1,0:T(8,128)S(1)}, f32[512,128]{1,0:T(8,128)}, u32[]{:S(2)}) copy-start(f32[512,128]{1,0:T(8,128)} %get-tuple-element.38) | copy-start | bytes 786436
  64.0 16.7 %copy-start.7 = (bf16[64,1024]{1,0:T(8,128)(2,1)S(1)}, bf16[64,1024]{1,0:T(8,128)(2,1)}, u32[]{:S(2)}) copy-start(bf16[64,1024]{1,0:T(8,128)(2,1)} %get-tuple-element.40) | copy-start | bytes 393220
  64.0 16.7 %copy-start.8 = (bf16[64,1024]{1,0:T(8,128)(2,1)S(1)}, bf16[64,1024]{1,0:T(8,128)(2,1)}, u32[]{:S(2)}) copy-start(bf16[64,1024]{1,0:T(8,128)(2,1)} %get-tuple-element.41) | copy-start | bytes 393220
  74.1 43.4 %all-to-all-start.2 = ((bf16[8,64,1152]{2,1,0:T(8,128)(2,1)}), bf16[8,64,1152]{2,1,0:T(8,128)(2,1)S(1)}, u32[]{:S(2)}, u32[]{:S(2)}) async-start(bf16[8,64,1152]{2,1,0:T(8,128)(2,1)} %convert_dynamic-update-slice_fusion), calls=%async_computation.2 | async-start | bytes 2359296 | tf_op jit(solution)/shard_map/all_to_all | solution.py:555
  80.8 36.7 %copy-start.2 = (s32[64]{0:T(128)S(1)}, s32[64]{0:T(128)}, u32[]{:S(2)}) copy-start(s32[64]{0:T(128)} %owner_ref.7) | copy-start | bytes 772
  80.8 36.7 %copy-start.3 = (f32[2048]{0:T(1024)S(1)}, f32[2048]{0:T(1024)}, u32[]{:S(2)}) copy-start(f32[2048]{0:T(1024)} %param.23) | copy-start | bytes 24580
  80.8 36.5 %collective-permute-start.4 = (bf16[64,2176]{1,0:T(8,128)(2,1)S(1)}, bf16[64,2176]{1,0:T(8,128)(2,1)S(1)}, u32[]{:S(2)}, u32[]{:S(2)}) collective-permute-start(bf16[64,2176]{1,0:T(8,128)(2,1)S(1)} %param.5), channel_id=1, source_target_pairs={{0,20},{4,24},{8,28},{12,0},{16,4},{20,8},{24,12},{28,16},{1,21},{... | collective-permute-start | bytes 835592 | tf_op jit(solution)/shard_map/cond/branch_5_fun/ppermute | solution.py:580

commit v2 on v1

--- a/solution.py
+++ b/solution.py
@@ -125,12 +125,34 @@
         body(slice(low, low + LANES))
 
 
+def write_shifts(shift_ref, mask_ref, ends, base, count):
+    mask_ref[...] = jnp.ones_like(mask_ref)
+    gap = jnp.zeros((1, LANES), F32)
+    for end in ends:
+        row = end - base + HALO
+
+        @pl.when((row >= 0) & (row < count + HALO))
+        def _(row=row):
+            for lag in range(1, SHORT):
+                for past in range(lag):
+                    mask_ref[lag - 1, pl.ds(row + past, 1), :] = gap
+
+    back = iota((CHUNK, LANES), 0) + 16 - iota((CHUNK, LANES), 1)
+    late = iota((CHUNK, 16), 0) + 16 - LANES - iota((CHUNK, 16), 1)
+    for lag in range(1, SHORT):
+        rows = slice((lag - 1) * CHUNK, lag * CHUNK)
+        for chunk in range(count // CHUNK):
+            mask = mask_ref[lag - 1, HALO + chunk * CHUNK : HALO + (chunk + 1) * CHUNK, :]
+            shift_ref[chunk, rows, :LANES] = jnp.where(back == lag, mask, 0.0).astype(BF16)
+            shift_ref[chunk, rows, LANES:] = jnp.where(late == lag, mask[:, :16], 0.0).astype(BF16)
+
+
 def mix_kernel(
     modes, size, ndoc,
     where_ref, lengths_ref,
     key_ref, value_ref, halo_ref, taps_ref, rates_ref,
     mixed_ref, state_ref,
-    mask_ref, tail_ref,
+    shift_ref, mask_ref, tail_ref,
 ):
     _, count, width = key_ref.shape
     chunks = count // CHUNK
@@ -139,17 +161,33 @@
     def _():
         base = where_ref[0] * count
         ends = running_ends(lengths_ref, ndoc)
-        write_lag_masks(mask_ref, ends, base, count)
+        write_shifts(shift_ref, mask_ref, ends, base, count)
         last = scalar_document(ends, base + count - 1).astype(F32)
         tail_ref[...] = jnp.where(row_documents(ends, base, count) == last, 1.0, 0.0).astype(F32)
 
+    def window(x_ref, which, start, lanes):
+        if start == 0:
+            halo = halo_ref[which, :, lanes].astype(F32)
+            ahead = jnp.concatenate([jnp.zeros((16 - HALO, LANES), F32), halo], 0).astype(BF16)
+        else:
+            ahead = x_ref[0, start - 16 : start, lanes]
+        return jnp.concatenate([ahead, x_ref[0, start : start + CHUNK, lanes]], 0)
+
     def tile(lanes):
         key_taps, value_taps = tap_rows(taps_ref, 1, lanes), tap_rows(taps_ref, 2, lanes)
-        for start in range(0, count, SPAN):
-            masks = lag_masks(mask_ref, start)
-            key = short_conv(extended(key_ref, halo_ref, 1, start, lanes), key_taps, masks)
-            value = short_conv(extended(value_ref, halo_ref, 2, start, lanes), value_taps, masks)
-            mixed_ref[start : start + SPAN, lanes] = (key * value).astype(BF16)
+        for chunk in range(chunks):
+            start = chunk * CHUNK
+            both = jnp.concatenate(
+                [window(key_ref, 1, start, lanes), window(value_ref, 2, start, lanes)], 1
+            )
+            moved = jnp.dot(shift_ref[chunk], both, preferred_element_type=F32)
+            key = key_ref[0, start : start + CHUNK, lanes].astype(F32) * key_taps[0]
+            value = value_ref[0, start : start + CHUNK, lanes].astype(F32) * value_taps[0]
+            for lag in range(1, SHORT):
+                rows = moved[(lag - 1) * CHUNK : lag * CHUNK]
+                key = key + rows[:, :LANES] * key_taps[lag]
+                value = value + rows[:, LANES:] * value_taps[lag]
+            mixed_ref[start : start + CHUNK, lanes] = (key * value).astype(BF16)
         rate = tile_rates(rates_ref.at[0], lanes.start, size)
         leave = jnp.exp(-rate * (CHUNK - 1 - iota((LANES, CHUNK), 1)).astype(F32))
         whole = jnp.exp(-rate * CHUNK)
@@ -398,7 +436,11 @@
             pl.BlockSpec((count, wide), lambda t, *_: (0, t)),
             pl.BlockSpec((copies, modes, wide), deep),
         ],
-        scratch_shapes=[pltpu.VMEM((3, count + 2 * HALO, LANES), F32), pltpu.VMEM((8, count), F32)],
+        scratch_shapes=[
+            pltpu.VMEM((count // CHUNK, (SHORT - 1) * CHUNK, CHUNK + 16), BF16),
+            pltpu.VMEM((SHORT - 1, count + 2 * HALO, LANES), F32),
+            pltpu.VMEM((8, count), F32),
+        ],
     )
     return pl.pallas_call(
         functools.partial(mix_kernel, modes, size, ndoc),

time: 121 us -> 119 us (0.983)
  the two profiles are of different devices: /device:TPU:8 before, /device:TPU:4 now
where the time goes in v2:
time: 119 us; the launch traced here: 118 us
  Pallas kernels  44 us (37%)
  waiting for transfers between devices  39 us (33%)
  starting transfers between devices  19.8 us (17%)
  blocking collectives  5.67 us (5%)
  local copies, waits for them, and re-layouts  5.39 us (5%)
  other arithmetic  2.57 us (2%)
  between operations  1.47 us (1%)
    ppermute x1, waiting for transfers between devices, moved(): lax.ppermute(value, 'ctx', [(s, (s + by) % nblocks) for s in range(nblock...  26.4 us
    pallas_call x2, Pallas kernels, conv(): pl.pallas_call(functools.partial(conv_kernel, modes, size, ndoc, nblocks,...  20.9 us
    all_to_all x3, starting transfers between devices, exchanged(): return lax.all_to_all(value, 'ctx', split_axis=0, concat_axis=0, tiled=True)  14.9 us
    pallas_call x1, Pallas kernels, mix(): pl.pallas_call(functools.partial(mix_kernel, modes, size, ndoc), grid_spe...  13.7 us
    all_to_all x3, waiting for transfers between devices, exchanged(): return lax.all_to_all(value, 'ctx', split_axis=0, concat_axis=0, tiled=True)  11 us
    pallas_call x1, Pallas kernels, add(): pl.pallas_call(functools.partial(add_kernel, modes, size, ndoc, nblocks),...  5.84 us
    psum x1, blocking collectives, on_device(): lax.psum(jnp.sum(squares + last_squares, 1), 'mp')  5.67 us
    pallas_call x1, Pallas kernels, norm(): pl.pallas_call(functools.partial(norm_kernel, len(blocks)), in_specs=[sme...  3.51 us
  transfers between devices with their start and end apart: 5, of which 5 were waited for; matrix products, arithmetic and copies ran while one was open for 5% of the time, Pallas kernels for 18%

profile of v2, /device:TPU:4, one launch (start us, length us, event | category | flops | bytes accessed | tf_op | source)
XLA Modules:
  0.0 118.0 jit_solution(1173613601110892249)
XLA Ops:
  0.0 0.9 slice.9
  0.9 3.4 %collective-permute-start.7 = (bf16[3,8,2048]{2,1,0:T(8,128)(2,1)S(1)}, bf16[3,8,2048]{2,1,0:T(8,128)(2,1)S(1)}, u32[]{:S(2)}, u32[]{:S(2)}) collective-permute-start(bf16[3,8,2048]{2,1,0:T(8,128)(2,1)S(1)} %slice.9), channel_id=1, source_target_pairs={{0,4},{4,8},{8,12},{12,16},{16,20},{20,24},{24,28},{1,5},{5,9},{9,... | collective-permute-start | bytes 294920 | tf_op jit(solution)/shard_map/ppermute | solution.py:583
  4.3 0.8 reshape.93
  5.7 1.7 %collective-permute-done.7.halo_ref.refs_1_ = bf16[3,8,2048]{2,1,0:T(8,128)(2,1)S(1)} collective-permute-done((bf16[3,8,2048]{2,1,0:T(8,128)(2,1)S(1)}, bf16[3,8,2048]{2,1,0:T(8,128)(2,1)S(1)}, u32[]{:S(2)}, u32[]{:S(2)}) %collective-permute-start.7) | collective-permute-done | bytes 98336 | tf_op jit(solution)/shard_map/ppermute | solution.py:583
  7.4 0.6 copy-done.5
  8.0 13.7 %mix.1 = (bf16[512,2048]{1,0:T(8,128)(2,1)}, bf16[8,16,2048]{2,1,0:T(8,128)(2,1)}) custom-call(s32[1]{0:T(128)} %bitcast.where_ref, s32[8]{0:T(128)} %lengths_ref.7, bf16[3,512,2048]{2,1,0:T(8,128)(2,1)} %bitcast.24, bf16[3,512,2048]{2,1,0:T(8,128)(2,1)} %bitcast.25, bf16[3,8,2048]{2,1,0:T(8,128)(2,1)} %copy-done.5, f32[3,7,2048]{2,1,0:T(8,128)} %refs_2_.3, ...), custom_call_target="tpu_custom_call" | custom-call | flops 62914560 | bytes 8388608 | tf_op jit(solution)/shard_map/mix/pallas_call | solution.py:445
  21.7 6.3 %all-to-all-start = ((bf16[8,16,2048]{2,1,0:T(8,128)(2,1)}), bf16[8,16,2048]{2,1,0:T(8,128)(2,1)S(1)}, u32[]{:S(2)}, u32[]{:S(2)}) async-start(bf16[8,16,2048]{2,1,0:T(8,128)(2,1)} %get-tuple-element.35), calls=%async_computation | async-start | bytes 1048576 | tf_op jit(solution)/shard_map/all_to_all | solution.py:597
  28.8 10.0 %conv.2 = (f32[512,1024]{1,0:T(8,128)}, bf16[512,1024]{1,0:T(8,128)(2,1)}) custom-call(s32[1]{0:T(128)} %bitcast.where_ref, s32[8]{0:T(128)} %lengths_ref.7, s32[64]{0:T(128)} %owner_ref.7, bf16[3,512,2048]{2,1,0:T(8,128)(2,1)} %bitcast.26, bf16[3,8,2048]{2,1,0:T(8,128)(2,1)} %copy-done.5, f32[3,7,2048]{2,1,0:T(8,128)} %refs_2_.3, ...), custom_call_target="tpu_custom_call" | custom-call | flops 1207959552 | bytes 4194304 | tf_op jit(solution)/shard_map/conv/pallas_call | solution.py:497
  38.8 2.0 %all-to-all-done.states_ref.refs_8_ = bf16[8,16,2048]{2,1,0:T(8,128)(2,1)S(1)} async-done(((bf16[8,16,2048]{2,1,0:T(8,128)(2,1)}), bf16[8,16,2048]{2,1,0:T(8,128)(2,1)S(1)}, u32[]{:S(2)}, u32[]{:S(2)}) %all-to-all-start) | async-done | bytes 524320 | tf_op jit(solution)/shard_map/all_to_all | solution.py:597
  40.8 0.8 copy-done.4
  41.6 5.8 %add.32 = (bf16[8,64,1024]{2,1,0:T(8,128)(2,1)}, bf16[64,1024]{1,0:T(8,128)(2,1)}, f32[512,128]{1,0:T(8,128)}) custom-call(s32[1]{0:T(128)} %bitcast.where_ref, s32[8]{0:T(128)} %lengths_ref.7, s32[64]{0:T(128)} %owner_ref.7, f32[512,1024]{1,0:T(8,128)} %get-tuple-element.33.base_ref, bf16[512,1024]{1,0:T(8,128)(2,1)} %get-tuple-element.34.gate_ref, ...), custom_call_target="tpu_custom_call" | custom-call | flops 157286400 | bytes 4194304 | tf_op jit(solution)/shard_map/add/pallas_call | solution.py:548
  47.5 4.2 %all-to-all-start.1 = ((bf16[8,64,1024]{2,1,0:T(8,128)(2,1)}), bf16[8,64,1024]{2,1,0:T(8,128)(2,1)S(1)}, u32[]{:S(2)}, u32[]{:S(2)}) async-start(bf16[8,64,1024]{2,1,0:T(8,128)(2,1)} %get-tuple-element.36), calls=%async_computation.1 | async-start | bytes 2097152 | tf_op jit(solution)/shard_map/all_to_all | solution.py:597
  51.9 0.7 select_reduce_fusion.2
  53.4 10.9 %conv.3 = (bf16[8,64,1152]{2,1,0:T(8,128)(2,1)}, bf16[64,1024]{1,0:T(8,128)(2,1)}, f32[512,128]{1,0:T(8,128)}) custom-call(s32[1]{0:T(128)} %bitcast.where_ref, s32[8]{0:T(128)} %lengths_ref.7, s32[64]{0:T(128)} %owner_ref.7, bf16[3,512,2048]{2,1,0:T(8,128)(2,1)} %bitcast.27, bf16[3,8,2048]{2,1,0:T(8,128)(2,1)} %copy-done.5, f32[3,7,2048]{2,1,0:T(8,128)} %refs_2_.3, ...), custom_call_target="tpu_custom_call" | custom-call | flops 1207959552 | bytes 4194304 | tf_op jit(solution)/shard_map/conv/pallas_call | solution.py:497
  64.4 1.1 add_reduce_fusion
  65.5 5.7 %psum.7 = f32[512]{0:T(512)S(1)} all-reduce(f32[512]{0:T(512)S(1)} %add_reduce_fusion), channel_id=1, replica_groups=mesh['ctx'=8,'mp'=4] {'mp'}, use_global_device_ids=true, to_apply=%region_3.4 | all-reduce | flops 512 | bytes 4096 | tf_op jit(solution)/shard_map/psum | solution.py:608
  71.8 0.7 convert_dynamic-update-slice_fusion
  72.5 3.6 %all-to-all-done.1.refs_0_ = bf16[8,64,1024]{2,1,0:T(8,128)(2,1)S(1)} async-done(((bf16[8,64,1024]{2,1,0:T(8,128)(2,1)}), bf16[8,64,1024]{2,1,0:T(8,128)(2,1)S(1)}, u32[]{:S(2)}, u32[]{:S(2)}) %all-to-all-start.1) | async-done | bytes 1048608 | tf_op jit(solution)/shard_map/all_to_all | solution.py:597
  76.1 4.3 %all-to-all-start.2 = ((bf16[8,64,1152]{2,1,0:T(8,128)(2,1)}), bf16[8,64,1152]{2,1,0:T(8,128)(2,1)S(1)}, u32[]{:S(2)}, u32[]{:S(2)}) async-start(bf16[8,64,1152]{2,1,0:T(8,128)(2,1)} %convert_dynamic-update-slice_fusion), calls=%async_computation.2 | async-start | bytes 2359296 | tf_op jit(solution)/shard_map/all_to_all | solution.py:597
  81.1 28.0 %conditional.1 = (bf16[64,2176]{1,0:T(8,128)(2,1)S(1)}) conditional(s32[]{:T(128)} %clamp.3, bf16[64,2176]{1,0:T(8,128)(2,1)S(1)} %pad_maximum_fusion, bf16[64,2176]{1,0:T(8,128)(2,1)S(1)} %pad_maximum_fusion, bf16[64,2176]{1,0:T(8,128)(2,1)S(1)} %pad_maximum_fusion, ...), branch_computations={%region_7.8_spmd, %region_8.9_spmd, %region_9.10_spmd, %region_10.... | conditional | bytes 1671216 | solution.py:624
  81.1 1.5 %collective-permute-start.1 = (bf16[64,2176]{1,0:T(8,128)(2,1)S(1)}, bf16[64,2176]{1,0:T(8,128)(2,1)S(1)}, u32[]{:S(2)}, u32[]{:S(2)}) collective-permute-start(bf16[64,2176]{1,0:T(8,128)(2,1)S(1)} %param.2), channel_id=1, source_target_pairs={{0,8},{4,12},{8,16},{12,20},{16,24},{20,28},{24,0},{28,4},{1,9},{5... | collective-permute-start | bytes 835592 | tf_op jit(solution)/shard_map/cond/branch_2_fun/ppermute | solution.py:622
  82.7 26.4 %collective-permute-done.1 = bf16[64,2176]{1,0:T(8,128)(2,1)S(1)} collective-permute-done((bf16[64,2176]{1,0:T(8,128)(2,1)S(1)}, bf16[64,2176]{1,0:T(8,128)(2,1)S(1)}, u32[]{:S(2)}, u32[]{:S(2)}) %collective-permute-start.1) | collective-permute-done | bytes 278560 | tf_op jit(solution)/shard_map/cond/branch_2_fun/ppermute | solution.py:622
  109.1 5.3 %all-to-all-done.2.refs_1_ = bf16[8,64,1152]{2,1,0:T(8,128)(2,1)S(1)} async-done(((bf16[8,64,1152]{2,1,0:T(8,128)(2,1)}), bf16[8,64,1152]{2,1,0:T(8,128)(2,1)S(1)}, u32[]{:S(2)}, u32[]{:S(2)}) %all-to-all-start.2) | async-done | bytes 1179680 | tf_op jit(solution)/shard_map/all_to_all | solution.py:597
  114.4 3.5 %norm.1 = bf16[512,2048]{1,0:T(8,128)(2,1)} custom-call(s32[1]{0:T(128)} %bitcast.where_ref, s32[64]{0:T(128)S(1)} %copy-done.2, bf16[8,64,1024]{2,1,0:T(8,128)(2,1)S(1)} %all-to-all-done.1.refs_0_, bf16[8,64,1152]{2,1,0:T(8,128)(2,1)S(1)} %all-to-all-done.2.refs_1_, bf16[64,2176]{1,0:T(8,128)(2,1)S(1)} %get-tuple-element.50.refs_2_, f32[1,2048]{1,0:T(1,128)S(1)} %bitcast.22), custom_call_target="tpu_custom_call" | custom-call | flops 3145728 | bytes 4194304 | tf_op jit(solution)/shard_map/norm/pallas_call | solution.py:563
  (34 shorter events, 2.3 us)
Async XLA Ops:
  0.9 6.5 %collective-permute-start.7 = (bf16[3,8,2048]{2,1,0:T(8,128)(2,1)S(1)}, bf16[3,8,2048]{2,1,0:T(8,128)(2,1)S(1)}, u32[]{:S(2)}, u32[]{:S(2)}) collective-permute-start(bf16[3,8,2048]{2,1,0:T(8,128)(2,1)S(1)} %slice.9), channel_id=1, source_target_pairs={{0,4},{4,8},{8,12},{12,16},{16,20},{20,24},{24,28},{1,5},{5,9},{9,... | collective-permute-start | bytes 294920 | tf_op jit(solution)/shard_map/ppermute | solution.py:583
  7.4 0.6 copy-start.5
  8.0 20.0 %copy-start.9 = (f32[128,16]{0,1:T(8,128)S(1)}, f32[128,16]{0,1:T(8,128)}, u32[]{:S(2)}) copy-start(f32[128,16]{0,1:T(8,128)} %param.21) | copy-start | bytes 24580
  8.0 20.7 %copy-start = (s32[64]{0:T(128)S(1)}, s32[64]{0:T(128)}, u32[]{:S(2)}) copy-start(s32[64]{0:T(128)} %owner_ref.7) | copy-start | bytes 772
  21.7 19.1 %all-to-all-start = ((bf16[8,16,2048]{2,1,0:T(8,128)(2,1)}), bf16[8,16,2048]{2,1,0:T(8,128)(2,1)S(1)}, u32[]{:S(2)}, u32[]{:S(2)}) async-start(bf16[8,16,2048]{2,1,0:T(8,128)(2,1)} %get-tuple-element.35), calls=%async_computation | async-start | bytes 1048576 | tf_op jit(solution)/shard_map/all_to_all | solution.py:597
  40.8 0.8 copy-start.4
  41.6 10.3 %copy-start.1 = (s32[64]{0:T(128)S(1)}, s32[64]{0:T(128)}, u32[]{:S(2)}) copy-start(s32[64]{0:T(128)} %owner_ref.7) | copy-start | bytes 772
  47.5 28.7 %all-to-all-start.1 = ((bf16[8,64,1024]{2,1,0:T(8,128)(2,1)}), bf16[8,64,1024]{2,1,0:T(8,128)(2,1)S(1)}, u32[]{:S(2)}, u32[]{:S(2)}) async-start(bf16[8,64,1024]{2,1,0:T(8,128)(2,1)} %get-tuple-element.36), calls=%async_computation.1 | async-start | bytes 2097152 | tf_op jit(solution)/shard_map/all_to_all | solution.py:597
  53.4 11.0 %copy-start.6 = (f32[512,128]{1,0:T(8,128)S(1)}, f32[512,128]{1,0:T(8,128)}, u32[]{:S(2)}) copy-start(f32[512,128]{1,0:T(8,128)} %get-tuple-element.38) | copy-start | bytes 786436
  64.3 16.7 %copy-start.7 = (bf16[64,1024]{1,0:T(8,128)(2,1)S(1)}, bf16[64,1024]{1,0:T(8,128)(2,1)}, u32[]{:S(2)}) copy-start(bf16[64,1024]{1,0:T(8,128)(2,1)} %get-tuple-element.40) | copy-start | bytes 393220
  64.3 16.7 %copy-start.8 = (bf16[64,1024]{1,0:T(8,128)(2,1)S(1)}, bf16[64,1024]{1,0:T(8,128)(2,1)}, u32[]{:S(2)}) copy-start(bf16[64,1024]{1,0:T(8,128)(2,1)} %get-tuple-element.41) | copy-start | bytes 393220
  76.1 38.3 %all-to-all-start.2 = ((bf16[8,64,1152]{2,1,0:T(8,128)(2,1)}), bf16[8,64,1152]{2,1,0:T(8,128)(2,1)S(1)}, u32[]{:S(2)}, u32[]{:S(2)}) async-start(bf16[8,64,1152]{2,1,0:T(8,128)(2,1)} %convert_dynamic-update-slice_fusion), calls=%async_computation.2 | async-start | bytes 2359296 | tf_op jit(solution)/shard_map/all_to_all | solution.py:597
  81.1 33.4 %copy-start.2 = (s32[64]{0:T(128)S(1)}, s32[64]{0:T(128)}, u32[]{:S(2)}) copy-start(s32[64]{0:T(128)} %owner_ref.7) | copy-start | bytes 772
  81.1 33.4 %copy-start.3 = (f32[2048]{0:T(1024)S(1)}, f32[2048]{0:T(1024)}, u32[]{:S(2)}) copy-start(f32[2048]{0:T(1024)} %param.23) | copy-start | bytes 24580
  81.1 27.9 %collective-permute-start.1 = (bf16[64,2176]{1,0:T(8,128)(2,1)S(1)}, bf16[64,2176]{1,0:T(8,128)(2,1)S(1)}, u32[]{:S(2)}, u32[]{:S(2)}) collective-permute-start(bf16[64,2176]{1,0:T(8,128)(2,1)S(1)} %param.2), channel_id=1, source_target_pairs={{0,8},{4,12},{8,16},{12,20},{16,24},{20,28},{24,0},{28,4},{1,9},{5... | collective-permute-start | bytes 835592 | tf_op jit(solution)/shard_map/cond/branch_2_fun/ppermute | solution.py:622

commit v3 on v2

--- a/solution.py
+++ b/solution.py
@@ -14,11 +14,13 @@
 HALO = 8
 EPS = 1e-06
 SPLIT = (4, 4)
+NEAR = 4
+ROOM = 16
 WIDE = 512
 SPAN = 64
 F32 = jnp.float32
 BF16 = jnp.bfloat16
-VMEM_LIMIT = 60 * 1024 * 1024
+VMEM_LIMIT = 64 * 1024 * 1024 - 256 * 1024
 
 
 def iota(shape, dim):
@@ -133,18 +135,21 @@
 
         @pl.when((row >= 0) & (row < count + HALO))
         def _(row=row):
-            for lag in range(1, SHORT):
+            for lag in range(1, NEAR + 1):
                 for past in range(lag):
                     mask_ref[lag - 1, pl.ds(row + past, 1), :] = gap
 
-    back = iota((CHUNK, LANES), 0) + 16 - iota((CHUNK, LANES), 1)
-    late = iota((CHUNK, 16), 0) + 16 - LANES - iota((CHUNK, 16), 1)
-    for lag in range(1, SHORT):
-        rows = slice((lag - 1) * CHUNK, lag * CHUNK)
-        for chunk in range(count // CHUNK):
-            mask = mask_ref[lag - 1, HALO + chunk * CHUNK : HALO + (chunk + 1) * CHUNK, :]
-            shift_ref[chunk, rows, :LANES] = jnp.where(back == lag, mask, 0.0).astype(BF16)
-            shift_ref[chunk, rows, LANES:] = jnp.where(late == lag, mask[:, :16], 0.0).astype(BF16)
+    reach = CHUNK + HALO
+    back = iota((reach, LANES), 0) + HALO - iota((reach, LANES), 1)
+    late = iota((reach, 16), 0) + HALO - LANES - iota((reach, 16), 1)
+    for chunk in range(count // CHUNK):
+        first, second = [], []
+        for lag in range(1, NEAR):
+            mask = mask_ref[lag - 1, chunk * CHUNK : chunk * CHUNK + reach, :]
+            first.append(jnp.where(back == lag, mask, 0.0))
+            second.append(jnp.where(late == lag, mask[:, :16], 0.0))
+        shift_ref[chunk, :, :LANES] = jnp.concatenate(first, 0).astype(BF16)
+        shift_ref[chunk, :, LANES:] = jnp.concatenate(second, 0).astype(BF16)
 
 
 def mix_kernel(
@@ -156,6 +161,7 @@
 ):
     _, count, width = key_ref.shape
     chunks = count // CHUNK
+    reach = CHUNK + HALO
 
     @pl.when(pl.program_id(0) == 0)
     def _():
@@ -173,20 +179,21 @@
             ahead = x_ref[0, start - 16 : start, lanes]
         return jnp.concatenate([ahead, x_ref[0, start : start + CHUNK, lanes]], 0)
 
+    def finish(here, moved, taps, apart):
+        rows = [here] + [moved[lag * reach : (lag + 1) * reach] for lag in range(NEAR - 1)]
+        far = sum(rows[lag] * taps[NEAR + lag] for lag in range(SHORT - NEAR))
+        far = pltpu.roll(far, NEAR, 0)[HALO:] * apart
+        return far + sum(row[HALO:] * taps[lag] for lag, row in enumerate(rows))
+
     def tile(lanes):
         key_taps, value_taps = tap_rows(taps_ref, 1, lanes), tap_rows(taps_ref, 2, lanes)
         for chunk in range(chunks):
             start = chunk * CHUNK
-            both = jnp.concatenate(
-                [window(key_ref, 1, start, lanes), window(value_ref, 2, start, lanes)], 1
-            )
-            moved = jnp.dot(shift_ref[chunk], both, preferred_element_type=F32)
-            key = key_ref[0, start : start + CHUNK, lanes].astype(F32) * key_taps[0]
-            value = value_ref[0, start : start + CHUNK, lanes].astype(F32) * value_taps[0]
-            for lag in range(1, SHORT):
-                rows = moved[(lag - 1) * CHUNK : lag * CHUNK]
-                key = key + rows[:, :LANES] * key_taps[lag]
-                value = value + rows[:, LANES:] * value_taps[lag]
+            keys, values = window(key_ref, 1, start, lanes), window(value_ref, 2, start, lanes)
+            moved = jnp.dot(shift_ref[chunk], jnp.concatenate([keys, values], 1), preferred_element_type=F32)
+            apart = mask_ref[NEAR - 1, HALO + start : HALO + start + CHUNK, :]
+            key = finish(keys.astype(F32)[16 - HALO :], moved[:, :LANES], key_taps, apart)
+            value = finish(values.astype(F32)[16 - HALO :], moved[:, LANES:], value_taps, apart)
             mixed_ref[start : start + CHUNK, lanes] = (key * value).astype(BF16)
         rate = tile_rates(rates_ref.at[0], lanes.start, size)
         leave = jnp.exp(-rate * (CHUNK - 1 - iota((LANES, CHUNK), 1)).astype(F32))
@@ -234,7 +241,8 @@
     squares_ref[start : start + SPAN, :] += summed * summed
     rounded = summed.astype(BF16)
     for b in range(SPAN // rows):
-        out_ref[slot_ref[start // rows + b], :, lanes] = rounded[b * rows : (b + 1) * rows]
+        tile = lanes.start // LANES * rows
+        out_ref[slot_ref[start // rows + b], tile : tile + rows, :] = rounded[b * rows : (b + 1) * rows]
 
 
 def conv_kernel(modes, size, ndoc, nblocks, carried, where_ref, lengths_ref, owner_ref, *refs):
@@ -322,7 +330,7 @@
 
     each_tile(width, tile)
     if carried:
-        spare_ref[...] = out_ref[refs[5][nblocks], :, :width]
+        spare_ref[...] = out_ref[refs[5][nblocks]]
 
 
 def add_kernel(
@@ -370,14 +378,15 @@
             hand_over(out_ref, squares_ref, slot_ref, summed, start, count // nblocks, lanes)
 
     each_tile(width, tile)
-    spare_ref[...] = out_ref[slot_ref[nblocks], :, :width]
+    spare_ref[...] = out_ref[slot_ref[nblocks]]
 
 
 def norm_kernel(parts, where_ref, owner_ref, *refs):
     blocks = refs[:parts]
     spare_ref, gain_ref, out_ref = refs[parts:]
-    nblocks, rows, _ = blocks[0].shape
     count, width = out_ref.shape
+    nblocks = blocks[0].shape[0]
+    rows = count // nblocks
     spare_block = jnp.int32(0)
     for i in range(nblocks):
         spare_block = jnp.where(is_second(owner_ref, nblocks, i), i, spare_block)
@@ -387,17 +396,17 @@
         is_spare = spare_block == i
         ahead = where_ref[0] - owner_ref[i]
         source = jnp.where(ahead < 0, ahead + nblocks, ahead)
-        halves = jnp.where(is_spare, spare_ref[:, width:].astype(F32), blocks[-1][source, :, -LANES:].astype(F32))
-        scale = halves[:, 0:1] + halves[:, 1:2]
-        low = 0
+        halves = jnp.where(is_spare, spare_ref[-ROOM:, :].astype(F32), blocks[-1][source, -ROOM:, :].astype(F32))[0:1]
+        scale = halves + pltpu.roll(jnp.broadcast_to(halves, (8, LANES)), LANES - rows, 1)[0:1]
+        scale = jnp.broadcast_to(scale, (LANES, LANES)).T[:rows]
+        tile = 0
         for part in range(parts):
-            share = min(blocks[part].shape[2], width - low)
-            for lane in range(0, share, LANES):
-                outs = slice(low + lane, low + lane + LANES)
-                value = blocks[part][source, :, lane : lane + LANES].astype(F32)
-                value = jnp.where(is_spare, spare_ref[:, outs].astype(F32), value)
+            for low in range(0, min(blocks[part].shape[1] // rows * rows, width // LANES * rows - tile * rows), rows):
+                outs = slice(tile * LANES, (tile + 1) * LANES)
+                value = blocks[part][source, low : low + rows, :].astype(F32)
+                value = jnp.where(is_spare, spare_ref[tile * rows : (tile + 1) * rows, :].astype(F32), value)
                 out_ref[rows_out, outs] = (value * scale * gain_ref[:, outs]).astype(BF16)
-            low += share
+                tile += 1
         return carry
 
     lax.fori_loop(0, nblocks, block, 0)
@@ -437,8 +446,8 @@
             pl.BlockSpec((copies, modes, wide), deep),
         ],
         scratch_shapes=[
-            pltpu.VMEM((count // CHUNK, (SHORT - 1) * CHUNK, CHUNK + 16), BF16),
-            pltpu.VMEM((SHORT - 1, count + 2 * HALO, LANES), F32),
+            pltpu.VMEM((count // CHUNK, (NEAR - 1) * (CHUNK + HALO), CHUNK + 16), BF16),
+            pltpu.VMEM((NEAR, count + 2 * HALO, LANES), F32),
             pltpu.VMEM((8, count), F32),
         ],
     )
@@ -509,13 +518,13 @@
 def handed(share, room, wide, count, nblocks):
     rows = count // nblocks
     specs = [
-        pl.BlockSpec((nblocks, rows, wide), lambda t, *_: (0, 0, t)),
-        pl.BlockSpec((rows, wide), lambda t, *_: (0, t)),
+        pl.BlockSpec((nblocks, wide // LANES * rows, LANES), lambda t, *_: (0, t, 0)),
+        pl.BlockSpec((wide // LANES * rows, LANES), lambda t, *_: (t, 0)),
         pl.BlockSpec((count, LANES), whole_array(2)),
     ]
     shapes = [
-        jax.ShapeDtypeStruct((nblocks, rows, share + room), BF16),
-        jax.ShapeDtypeStruct((rows, share), BF16),
+        jax.ShapeDtypeStruct((nblocks, share // LANES * rows + room, LANES), BF16),
+        jax.ShapeDtypeStruct((share // LANES * rows, LANES), BF16),
         jax.ShapeDtypeStruct((count, LANES), F32),
     ]
     return specs, shapes
@@ -555,9 +564,8 @@
     )(*scalars, base, gate, by_step(rates, wide, size), by_step(residues, wide, size), states)
 
 
-def norm(where, owner, blocks, spare, gain):
-    nblocks, rows, _ = blocks[0].shape
-    count, width = nblocks * rows, gain.shape[1]
+def norm(where, owner, blocks, spare, gain, count):
+    width = gain.shape[1]
     vmem = pl.BlockSpec(memory_space=pltpu.VMEM)
     smem = pl.BlockSpec(memory_space=pltpu.SMEM)
     return pl.pallas_call(
@@ -604,25 +612,25 @@
     base, gate = conv(0, first, 0, *shared, None, size, ndoc, nblocks)
     out, spare, squares = add(scalars, base, gate, rates, residues, states, size, ndoc, nblocks)
     block = exchanged(out)
-    out, last_spare, last_squares = conv(first, second, LANES, *shared, states, size, ndoc, nblocks)
+    out, last_spare, last_squares = conv(first, second, ROOM, *shared, states, size, ndoc, nblocks)
     mean = lax.psum(jnp.sum(squares + last_squares, 1), "mp") / (width * lax.axis_size("mp"))
     inverse = lax.rsqrt(mean + EPS)
     high = lax.reduce_precision(inverse, 8, 7)
-    column = iota((count, LANES), 1)
-    halves = jnp.where(column == 0, high[:, None], jnp.where(column == 1, (inverse - high)[:, None], 0.0))
-    halves = halves.reshape(nblocks, rows, LANES)
+    halves = jnp.concatenate([high.reshape(nblocks, rows), (inverse - high).reshape(nblocks, rows)], 1)
+    halves = jnp.pad(halves, ((0, 0), (0, LANES - 2 * rows)))
     in_slot = slots[None, :] == ids[:, None]
-    by_slot = jnp.sum(jnp.where(in_slot[:, :, None, None], halves[None], 0.0), 1).astype(BF16)
-    spare_halves = jnp.sum(jnp.where(twice[:, None, None], halves, 0.0), 0).astype(BF16)
-    out = lax.dynamic_update_slice(out, by_slot, (0, 0, second))
+    by_slot = jnp.sum(jnp.where(in_slot[:, :, None], halves[None], 0.0), 1)
+    by_slot = jnp.broadcast_to(by_slot.astype(BF16)[:, None], (nblocks, ROOM, LANES))
+    spare_halves = jnp.sum(jnp.where(twice[:, None], halves, 0.0), 0).astype(BF16)
+    out = lax.dynamic_update_slice(out, by_slot, (0, second // LANES * rows, 0))
     blocks = [block, exchanged(out)]
-    spares = jnp.concatenate([spare, last_spare, spare_halves], 1)
+    spares = jnp.concatenate([spare, last_spare, jnp.broadcast_to(spare_halves[None], (ROOM, LANES))], 0)
 
     def moved(by):
         return lambda value: lax.ppermute(value, "ctx", [(s, (s + by) % nblocks) for s in range(nblocks)])
 
     spare = lax.switch(spare_shift, [lambda value: value] + [moved(d) for d in range(1, nblocks)], spares)
-    return norm(scalars[0], owner, blocks, spare, gain.reshape(1, width))
+    return norm(scalars[0], owner, blocks, spare, gain.reshape(1, width), count)
 
 
 def solution(mesh):

time: 119 us -> 121 us (1.017)
  waiting for transfers between devices: 39 us -> 41.2 us
  starting transfers between devices: 19.8 us -> 21.9 us
    ppermute x1, waiting for transfers between devices: 26.4 us -> 33.3 us  [moved(): lax.ppermute(value, 'ctx', [(s, (s + by) % nblocks) for s in range(nblock...]
    all_to_all x3, waiting for transfers between devices: 11 us -> 6.25 us  [exchanged(): return lax.all_to_all(value, 'ctx', split_axis=0, concat_axis=0, tiled=True)]
    ppermute x1, starting transfers between devices: 1.53 us -> 3.35 us  [moved(): lax.ppermute(value, 'ctx', [(s, (s + by) % nblocks) for s in range(nblock...]
    pallas_call x1, Pallas kernels: 13.7 us -> 12.2 us  [mix(): pl.pallas_call(functools.partial(mix_kernel, modes, size, ndoc), grid_spe...]
  transfers between devices with their start and end apart: 5 -> 5, of which waited for: 5 -> 4; matrix products, arithmetic and copies ran while one was open for 5% -> 4% of each run, Pallas kernels for 18% -> 17%
where the time goes in v3:
time: 121 us; the launch traced here: 120 us
  Pallas kernels  42.8 us (35%)
  waiting for transfers between devices  41.2 us (34%)
  starting transfers between devices  21.9 us (18%)
  blocking collectives  5.67 us (5%)
  local copies, waits for them, and re-layouts  4.54 us (4%)
  other arithmetic  2.35 us (2%)
  between operations  1.47 us (1%)
    ppermute x1, waiting for transfers between devices, moved(): lax.ppermute(value, 'ctx', [(s, (s + by) % nblocks) for s in range(nblock...  33.3 us
    pallas_call x2, Pallas kernels, conv(): pl.pallas_call(functools.partial(conv_kernel, modes, size, ndoc, nblocks,...  20.7 us
    all_to_all x3, starting transfers between devices, exchanged(): return lax.all_to_all(value, 'ctx', split_axis=0, concat_axis=0, tiled=True)  15.1 us
    pallas_call x1, Pallas kernels, mix(): pl.pallas_call(functools.partial(mix_kernel, modes, size, ndoc), grid_spe...  12.2 us
    all_to_all x3, waiting for transfers between devices, exchanged(): return lax.all_to_all(value, 'ctx', split_axis=0, concat_axis=0, tiled=True)  6.25 us
    pallas_call x1, Pallas kernels, add(): pl.pallas_call(functools.partial(add_kernel, modes, size, ndoc, nblocks),...  5.74 us
    psum x1, blocking collectives, on_device(): lax.psum(jnp.sum(squares + last_squares, 1), 'mp')  5.67 us
    pallas_call x1, Pallas kernels, norm(): pl.pallas_call(functools.partial(norm_kernel, len(blocks)), in_specs=[sme...  4.24 us
  transfers between devices with their start and end apart: 5, of which 4 were waited for; matrix products, arithmetic and copies ran while one was open for 4% of the time, Pallas kernels for 17%

profile of v3, /device:TPU:4, one launch (start us, length us, event | category | flops | bytes accessed | tf_op | source)
XLA Modules:
  0.0 120.0 jit_solution(13270316252662977699)
XLA Ops:
  0.0 0.9 slice.9
  0.9 3.4 %collective-permute-start.7 = (bf16[3,8,2048]{2,1,0:T(8,128)(2,1)S(1)}, bf16[3,8,2048]{2,1,0:T(8,128)(2,1)S(1)}, u32[]{:S(2)}, u32[]{:S(2)}) collective-permute-start(bf16[3,8,2048]{2,1,0:T(8,128)(2,1)S(1)} %slice.9), channel_id=1, source_target_pairs={{0,4},{4,8},{8,12},{12,16},{16,20},{20,24},{24,28},{1,5},{5,9},{9,... | collective-permute-start | bytes 294920 | tf_op jit(solution)/shard_map/ppermute | solution.py:591
  4.3 0.8 reshape.63
  5.1 0.6 copy.17
  5.7 1.7 %collective-permute-done.7.halo_ref.refs_1_ = bf16[3,8,2048]{2,1,0:T(8,128)(2,1)S(1)} collective-permute-done((bf16[3,8,2048]{2,1,0:T(8,128)(2,1)S(1)}, bf16[3,8,2048]{2,1,0:T(8,128)(2,1)S(1)}, u32[]{:S(2)}, u32[]{:S(2)}) %collective-permute-start.7) | collective-permute-done | bytes 98336 | tf_op jit(solution)/shard_map/ppermute | solution.py:591
  7.4 0.6 copy-done.3
  8.0 12.2 %mix.1 = (bf16[512,2048]{1,0:T(8,128)(2,1)}, bf16[8,16,2048]{2,1,0:T(8,128)(2,1)}) custom-call(s32[1]{0:T(128)} %bitcast.where_ref, s32[8]{0:T(128)} %lengths_ref.7, bf16[3,512,2048]{2,1,0:T(8,128)(2,1)} %bitcast.24, bf16[3,512,2048]{2,1,0:T(8,128)(2,1)} %bitcast.25, bf16[3,8,2048]{2,1,0:T(8,128)(2,1)} %copy-done.3, f32[3,7,2048]{2,1,0:T(8,128)} %refs_2_.3, ...), custom_call_target="tpu_custom_call" | custom-call | flops 62914560 | bytes 8388608 | tf_op jit(solution)/shard_map/mix/pallas_call | solution.py:454
  20.2 6.3 %all-to-all-start = ((bf16[8,16,2048]{2,1,0:T(8,128)(2,1)}), bf16[8,16,2048]{2,1,0:T(8,128)(2,1)}, u32[]{:S(2)}, u32[]{:S(2)}) async-start(bf16[8,16,2048]{2,1,0:T(8,128)(2,1)} %get-tuple-element.35), calls=%async_computation | async-start | bytes 1048576 | tf_op jit(solution)/shard_map/all_to_all | solution.py:605
  26.7 0.6 copy.16
  27.3 10.0 %conv.2 = (f32[512,1024]{1,0:T(8,128)}, bf16[512,1024]{1,0:T(8,128)(2,1)}) custom-call(s32[1]{0:T(128)} %bitcast.where_ref, s32[8]{0:T(128)} %lengths_ref.7, s32[64]{0:T(128)} %owner_ref.7, bf16[3,512,2048]{2,1,0:T(8,128)(2,1)} %bitcast.26, bf16[3,8,2048]{2,1,0:T(8,128)(2,1)} %copy-done.3, f32[3,7,2048]{2,1,0:T(8,128)} %refs_2_.3, ...), custom_call_target="tpu_custom_call" | custom-call | flops 1207959552 | bytes 4194304 | tf_op jit(solution)/shard_map/conv/pallas_call | solution.py:506
  37.3 2.2 %all-to-all-done.states_ref.refs_8_ = bf16[8,16,2048]{2,1,0:T(8,128)(2,1)} async-done(((bf16[8,16,2048]{2,1,0:T(8,128)(2,1)}), bf16[8,16,2048]{2,1,0:T(8,128)(2,1)}, u32[]{:S(2)}, u32[]{:S(2)}) %all-to-all-start) | async-done | bytes 524320 | tf_op jit(solution)/shard_map/all_to_all | solution.py:605
  39.5 5.7 %add.32 = (bf16[8,512,128]{2,1,0:T(8,128)(2,1)}, bf16[512,128]{1,0:T(8,128)(2,1)}, f32[512,128]{1,0:T(8,128)}) custom-call(s32[1]{0:T(128)} %bitcast.where_ref, s32[8]{0:T(128)} %lengths_ref.7, s32[64]{0:T(128)} %owner_ref.7, f32[512,1024]{1,0:T(8,128)} %get-tuple-element.33.base_ref, bf16[512,1024]{1,0:T(8,128)(2,1)} %get-tuple-element.34.gate_ref, ...), custom_call_target="tpu_custom_call" | custom-call | flops 157286400 | bytes 4194304 | tf_op jit(solution)/shard_map/add/pallas_call | solution.py:557
  45.2 4.5 %all-to-all-start.1 = ((bf16[8,512,128]{2,1,0:T(8,128)(2,1)}), bf16[8,512,128]{2,1,0:T(8,128)(2,1)}, u32[]{:S(2)}, u32[]{:S(2)}) async-start(bf16[8,512,128]{2,1,0:T(8,128)(2,1)} %get-tuple-element.36), calls=%async_computation.1 | async-start | bytes 2097152 | tf_op jit(solution)/shard_map/all_to_all | solution.py:605
  50.0 0.7 select_reduce_fusion.2
  51.3 10.7 %conv.3 = (bf16[8,528,128]{2,1,0:T(8,128)(2,1)}, bf16[512,128]{1,0:T(8,128)(2,1)}, f32[512,128]{1,0:T(8,128)}) custom-call(s32[1]{0:T(128)} %bitcast.where_ref, s32[8]{0:T(128)} %lengths_ref.7, s32[64]{0:T(128)} %owner_ref.7, bf16[3,512,2048]{2,1,0:T(8,128)(2,1)} %bitcast.27, bf16[3,8,2048]{2,1,0:T(8,128)(2,1)} %copy-done.3, f32[3,7,2048]{2,1,0:T(8,128)} %refs_2_.3, ...), custom_call_target="tpu_custom_call" | custom-call | flops 1207959552 | bytes 4194304 | tf_op jit(solution)/shard_map/conv/pallas_call | solution.py:506
  62.1 1.2 %add_reduce_fusion = f32[512]{0:T(512)S(1)} fusion(f32[512,128]{1,0:T(8,128)} %get-tuple-element.38, f32[512,128]{1,0:T(8,128)} %get-tuple-element.39), kind=kLoop, calls=%fused_computation.1 | loop fusion | flops 130560 | bytes 526336 | tf_op jit(solution)/shard_map/reduce_sum | solution.py:616
  63.3 5.7 %psum.7 = f32[512]{0:T(512)S(1)} all-reduce(f32[512]{0:T(512)S(1)} %add_reduce_fusion), channel_id=1, replica_groups=mesh['ctx'=8,'mp'=4] {'mp'}, use_global_device_ids=true, to_apply=%region_3.4 | all-reduce | flops 512 | bytes 4096 | tf_op jit(solution)/shard_map/psum | solution.py:616
  69.3 0.6 broadcast_dynamic-update-slice_fusion
  69.9 4.0 %all-to-all-done.1.refs_0_ = bf16[8,512,128]{2,1,0:T(8,128)(2,1)} async-done(((bf16[8,512,128]{2,1,0:T(8,128)(2,1)}), bf16[8,512,128]{2,1,0:T(8,128)(2,1)}, u32[]{:S(2)}, u32[]{:S(2)}) %all-to-all-start.1) | async-done | bytes 1048608 | tf_op jit(solution)/shard_map/all_to_all | solution.py:605
  74.0 4.3 %all-to-all-start.2 = ((bf16[8,528,128]{2,1,0:T(8,128)(2,1)}), bf16[8,528,128]{2,1,0:T(8,128)(2,1)S(1)}, u32[]{:S(2)}, u32[]{:S(2)}) async-start(bf16[8,528,128]{2,1,0:T(8,128)(2,1)} %broadcast_dynamic-update-slice_fusion), calls=%async_computation.2 | async-start | bytes 2162688 | tf_op jit(solution)/shard_map/all_to_all | solution.py:605
  79.0 36.7 %conditional.1 = (bf16[1040,128]{1,0:T(8,128)(2,1)S(1)}) conditional(s32[]{:T(128)} %clamp.3, bf16[1040,128]{1,0:T(8,128)(2,1)S(1)} %pad_maximum_fusion, bf16[1040,128]{1,0:T(8,128)(2,1)S(1)} %pad_maximum_fusion, bf16[1040,128]{1,0:T(8,128)(2,1)S(1)} %pad_maximum_fusion, ...), branch_computations={%region_7.8_spmd, %region_8.9_spmd, %region_9.10_spmd, %region_10.... | conditional | bytes 1597488 | solution.py:632
  79.1 3.3 %collective-permute-start.4 = (bf16[1040,128]{1,0:T(8,128)(2,1)S(1)}, bf16[1040,128]{1,0:T(8,128)(2,1)S(1)}, u32[]{:S(2)}, u32[]{:S(2)}) collective-permute-start(bf16[1040,128]{1,0:T(8,128)(2,1)S(1)} %param.5), channel_id=1, source_target_pairs={{0,20},{4,24},{8,28},{12,0},{16,4},{20,8},{24,12},{28,16},{1,21},{... | collective-permute-start | bytes 798728 | tf_op jit(solution)/shard_map/cond/branch_5_fun/ppermute | solution.py:630
  82.4 33.3 %collective-permute-done.4 = bf16[1040,128]{1,0:T(8,128)(2,1)S(1)} collective-permute-done((bf16[1040,128]{1,0:T(8,128)(2,1)S(1)}, bf16[1040,128]{1,0:T(8,128)(2,1)S(1)}, u32[]{:S(2)}, u32[]{:S(2)}) %collective-permute-start.4) | collective-permute-done | bytes 266272 | tf_op jit(solution)/shard_map/cond/branch_5_fun/ppermute | solution.py:630
  115.8 4.2 %norm.1 = bf16[512,2048]{1,0:T(8,128)(2,1)} custom-call(s32[1]{0:T(128)} %bitcast.where_ref, s32[64]{0:T(128)S(1)} %copy-done.1, bf16[8,512,128]{2,1,0:T(8,128)(2,1)} %all-to-all-done.1.refs_0_, bf16[8,528,128]{2,1,0:T(8,128)(2,1)S(1)} %all-to-all-done.2.refs_1_, bf16[1040,128]{1,0:T(8,128)(2,1)S(1)} %get-tuple-element.48.refs_2_, f32[1,2048]{1,0:T(1,128)S(1)} %bitcast.22), custom_call_target="tpu_custom_call" | custom-call | flops 3145728 | bytes 4194304 | tf_op jit(solution)/shard_map/norm/pallas_call | solution.py:571
  (28 shorter events, 0.8 us)
Async XLA Ops:
  0.9 6.5 %collective-permute-start.7 = (bf16[3,8,2048]{2,1,0:T(8,128)(2,1)S(1)}, bf16[3,8,2048]{2,1,0:T(8,128)(2,1)S(1)}, u32[]{:S(2)}, u32[]{:S(2)}) collective-permute-start(bf16[3,8,2048]{2,1,0:T(8,128)(2,1)S(1)} %slice.9), channel_id=1, source_target_pairs={{0,4},{4,8},{8,12},{12,16},{16,20},{20,24},{24,28},{1,5},{5,9},{9,... | collective-permute-start | bytes 294920 | tf_op jit(solution)/shard_map/ppermute | solution.py:591
  7.4 0.6 copy-start.3
  8.0 18.5 %copy-start.6 = (f32[128,16]{0,1:T(8,128)S(1)}, f32[128,16]{0,1:T(8,128)}, u32[]{:S(2)}) copy-start(f32[128,16]{0,1:T(8,128)} %param.21) | copy-start | bytes 24580
  20.2 19.2 %all-to-all-start = ((bf16[8,16,2048]{2,1,0:T(8,128)(2,1)}), bf16[8,16,2048]{2,1,0:T(8,128)(2,1)}, u32[]{:S(2)}, u32[]{:S(2)}) async-start(bf16[8,16,2048]{2,1,0:T(8,128)(2,1)} %get-tuple-element.35), calls=%async_computation | async-start | bytes 1048576 | tf_op jit(solution)/shard_map/all_to_all | solution.py:605
  39.5 10.2 %copy-start = (s32[64]{0:T(128)S(1)}, s32[64]{0:T(128)}, u32[]{:S(2)}) copy-start(s32[64]{0:T(128)} %owner_ref.7) | copy-start | bytes 772
  45.2 28.8 %all-to-all-start.1 = ((bf16[8,512,128]{2,1,0:T(8,128)(2,1)}), bf16[8,512,128]{2,1,0:T(8,128)(2,1)}, u32[]{:S(2)}, u32[]{:S(2)}) async-start(bf16[8,512,128]{2,1,0:T(8,128)(2,1)} %get-tuple-element.36), calls=%async_computation.1 | async-start | bytes 2097152 | tf_op jit(solution)/shard_map/all_to_all | solution.py:605
  62.0 16.9 %copy-start.4 = (bf16[512,128]{1,0:T(8,128)(2,1)S(1)}, bf16[512,128]{1,0:T(8,128)(2,1)}, u32[]{:S(2)}) copy-start(bf16[512,128]{1,0:T(8,128)(2,1)} %get-tuple-element.40) | copy-start | bytes 393220
  62.0 16.9 %copy-start.5 = (bf16[512,128]{1,0:T(8,128)(2,1)S(1)}, bf16[512,128]{1,0:T(8,128)(2,1)}, u32[]{:S(2)}) copy-start(bf16[512,128]{1,0:T(8,128)(2,1)} %get-tuple-element.41) | copy-start | bytes 393220
  74.0 41.8 %all-to-all-start.2 = ((bf16[8,528,128]{2,1,0:T(8,128)(2,1)}), bf16[8,528,128]{2,1,0:T(8,128)(2,1)S(1)}, u32[]{:S(2)}, u32[]{:S(2)}) async-start(bf16[8,528,128]{2,1,0:T(8,128)(2,1)} %broadcast_dynamic-update-slice_fusion), calls=%async_computation.2 | async-start | bytes 2162688 | tf_op jit(solution)/shard_map/all_to_all | solution.py:605
  79.0 36.8 %copy-start.1 = (s32[64]{0:T(128)S(1)}, s32[64]{0:T(128)}, u32[]{:S(2)}) copy-start(s32[64]{0:T(128)} %owner_ref.7) | copy-start | bytes 772
  79.0 36.8 %copy-start.2 = (f32[2048]{0:T(1024)S(1)}, f32[2048]{0:T(1024)}, u32[]{:S(2)}) copy-start(f32[2048]{0:T(1024)} %param.23) | copy-start | bytes 24580
  79.1 36.6 %collective-permute-start.4 = (bf16[1040,128]{1,0:T(8,128)(2,1)S(1)}, bf16[1040,128]{1,0:T(8,128)(2,1)S(1)}, u32[]{:S(2)}, u32[]{:S(2)}) collective-permute-start(bf16[1040,128]{1,0:T(8,128)(2,1)S(1)} %param.5), channel_id=1, source_target_pairs={{0,20},{4,24},{8,28},{12,0},{16,4},{20,8},{24,12},{28,16},{1,21},{... | collective-permute-start | bytes 798728 | tf_op jit(solution)/shard_map/cond/branch_5_fun/ppermute | solution.py:630
